TPU v7x, 128 devices: a whole 4x4x4 slice. The times are simulated.
128 devices in a mesh: rep: 4 (over z_lo, core), ctx: 16 (over x, y), tp: 2 (over z_hi).
Axes of the slice: x: 4, y: 4, z: 4 (z_hi: 2, z_lo: 2; z = z_hi * 2 + z_lo), core: 2. Of those that a mesh axis runs over, the one named last changes fastest.
Arguments:
- tokens: bfloat16 [8, 1024, 1024], P('rep', 'ctx'), may hold values from -6 to 6
- cotangent: bfloat16 [8, 1024, 1024], P('rep', 'ctx'), may hold values from -6 to 6
- segments: int32 [8, 1024], P('rep'), may hold values from 0 to 3, as said below
- w_query: bfloat16 [1, 1024, 2048], P(None, 'ctx', 'tp'), may hold values from -0.1875 to 0.1875
- w_key: bfloat16 [1, 1024, 1024], P(None, 'ctx', 'tp'), may hold values from -0.1875 to 0.1875
- w_value: bfloat16 [1, 1024, 1024], P(None, 'ctx', 'tp'), may hold values from -0.1875 to 0.1875
- w_output: bfloat16 [1, 2048, 1024], P(None, 'tp', 'ctx'), may hold values from -0.75 to 0.75
- w_gate: bfloat16 [1, 1024, 3072], P(None, 'ctx', 'tp'), may hold values from -0.1875 to 0.1875
- w_up: bfloat16 [1, 1024, 3072], P(None, 'ctx', 'tp'), may hold values from -0.1875 to 0.1875
- w_down: bfloat16 [1, 3072, 1024], P(None, 'tp', 'ctx'), may hold values from -0.109375 to 0.109375
- norm_attn: bfloat16 [1, 1024], P(None, 'ctx'), may hold values from 0.25 to 1.75
- norm_mlp: bfloat16 [1, 1024], P(None, 'ctx'), may hold values from 0.25 to 1.75
- norm_query: bfloat16 [1, 128], P(None, 'ctx'), may hold values from 0.25 to 1.75
- norm_key: bfloat16 [1, 128], P(None, 'ctx'), may hold values from 0.25 to 1.75
Outputs:
- out_tokens: float32 [8, 1024, 1024], P('rep', 'ctx')
- tokens_grad: float32 [8, 1024, 1024], P('rep', 'ctx')
- w_query_grad: float32 [1, 1024, 2048], P(None, 'ctx', 'tp')
- w_key_grad: float32 [1, 1024, 1024], P(None, 'ctx', 'tp')
- w_value_grad: float32 [1, 1024, 1024], P(None, 'ctx', 'tp')
- w_output_grad: float32 [1, 2048, 1024], P(None, 'tp', 'ctx')
- w_gate_grad: float32 [1, 1024, 3072], P(None, 'ctx', 'tp')
- w_up_grad: float32 [1, 1024, 3072], P(None, 'ctx', 'tp')
- w_down_grad: float32 [1, 3072, 1024], P(None, 'tp', 'ctx')
- norm_attn_grad: float32 [1, 1024], P(None, 'ctx')
- norm_mlp_grad: float32 [1, 1024], P(None, 'ctx')
- norm_query_grad: float32 [1, 128], P(None, 'ctx')
- norm_key_grad: float32 [1, 128], P(None, 'ctx')
Inputs may be any that keep to these rules, and one draw needn't show every extreme that they name: `segments`: within each sequence the ids start at 0, never fall and rise by one at each new document; every document has 200 tokens or more. In each group of 2 consecutive sequences one sequence, drawn from the seed, is a single document and another holds four.
All inputs are finite; a program needn't handle non-finite values.
Results may differ from a plain program's by a relative error of at most 0.017.
Values may be sent and summed in bfloat16 or wider, within the bound.
No kernel may reach another device: no remote copies, remote signals or barrier semaphores. Data moves between devices by JAX's collectives and lax.ppermute only.
A program may use at most 128 MiB of HBM per device.

v0:
```python
import math

import jax
import jax.numpy as jnp
from jax import lax
from jax.experimental import pallas as pl
from jax.experimental.pallas import tpu as pltpu
from jax.sharding import PartitionSpec as P

HD = 128
D = 1024
SCALE = 1.0 / math.sqrt(HD)
norm_eps = 1e-06
rope_base = 1000000.0
masked_score = -1e30
bf16 = jnp.bfloat16
f32 = jnp.float32


def core_swap(values):
    return lax.ppermute(values, "rep", [(0, 1), (1, 0), (2, 3), (3, 2)])


def zlo_swap(values):
    return lax.ppermute(values, "rep", [(0, 2), (1, 3), (2, 0), (3, 1)])


def tp_swap(values):
    return lax.ppermute(values, "tp", [(0, 1), (1, 0)])


def exchange(values):
    return lax.all_to_all(values, "ctx", 0, 0, tiled=True)


def mm(left, right):
    return jnp.dot(left, right, preferred_element_type=f32)


def mm_nt(left, right):
    return lax.dot_general(left, right, (((1,), (1,)), ((), ())), preferred_element_type=f32)


def mm_tn(left, right):
    return lax.dot_general(left, right, (((0,), (0,)), ((), ())), preferred_element_type=f32)


def rms_norm(values):
    return values * lax.rsqrt(jnp.mean(values * values, -1, keepdims=True) + norm_eps)


def norm_back(values, gain, upstream):
    inverse = lax.rsqrt(jnp.mean(values * values, -1, keepdims=True) + norm_eps)
    normed = values * inverse
    scaled = upstream * gain
    value_grad = inverse * (scaled - normed * jnp.mean(scaled * normed, -1, keepdims=True))
    return value_grad, jnp.sum(upstream * normed, 0, keepdims=True)


def rotate(values, cosine, sine):
    return values * cosine + pltpu.roll(values, HD // 2, 1) * sine


def rotate_back(values, cosine, sine):
    return values * cosine - pltpu.roll(values, HD // 2, 1) * sine


def kernel_call(body, out_shape, flops, *operands):
    return kernel_call_scratch(body, out_shape, [], flops, *operands)


def kernel_call_scratch(body, out_shape, scratch, flops, *operands):
    specs = [pl.BlockSpec(memory_space=pltpu.SMEM)]
    specs += [pl.BlockSpec(memory_space=pltpu.VMEM)] * (len(operands) - 1)
    size = sum(math.prod(x.shape) * x.dtype.itemsize for x in list(operands) + list(out_shape))
    return pl.pallas_call(
        body,
        out_shape=out_shape,
        in_specs=specs,
        out_specs=[pl.BlockSpec(memory_space=pltpu.VMEM)] * len(out_shape),
        scratch_shapes=scratch,
        cost_estimate=pl.CostEstimate(flops=flops, bytes_accessed=size, transcendentals=0),
        compiler_params=pltpu.CompilerParams(vmem_limit_bytes=48 << 20),
    )(*operands)


def shape(dims, dtype):
    return jax.ShapeDtypeStruct(dims, dtype)


BLOCK = 256


def masked_scores(queries, keys, seg_column, seg_row, start, length):
    row = start + lax.broadcasted_iota(jnp.int32, (BLOCK, length), 0)
    column = lax.broadcasted_iota(jnp.int32, (BLOCK, length), 1)
    allowed = (seg_column == seg_row) & (column <= row)
    return jnp.where(allowed, mm_nt(queries, keys) * SCALE, masked_score)


def attend_kernel(odd, q_ref, own_ref, other_ref, segc_ref, segr_ref, mixed_ref, lse_ref):
    own, other = own_ref[...], other_ref[...]
    flag = odd[0] == 1
    keys, values = jnp.where(flag, other, own), jnp.where(flag, own, other)
    for start in range(0, 1024, BLOCK):
        rows = slice(start, start + BLOCK)
        length = start + BLOCK
        scores = masked_scores(
            q_ref[rows], keys[:length], segc_ref[rows], segr_ref[:, :length], start, length
        )
        row_max = jnp.max(scores, -1, keepdims=True)
        weights_exp = jnp.exp(scores - row_max)
        row_total = jnp.sum(weights_exp, -1, keepdims=True)
        probs = (weights_exp * (1.0 / row_total)).astype(bf16)
        mixed_ref[rows] = mm(probs, values[:length]).astype(bf16)
        lse_ref[rows] = row_max + jnp.log(row_total)


def attend_back_kernel(
    odd,
    q_ref,
    own_ref,
    other_ref,
    segc_ref,
    segr_ref,
    lse_ref,
    up_ref,
    raw_ref,
    gain_ref,
    cos_ref,
    sin_ref,
    keep_ref,
    give_ref,
    low_ref,
    gain_grad_ref,
    key_sum,
    value_sum,
):
    own, other = own_ref[...], other_ref[...]
    flag = odd[0] == 1
    keys, values = jnp.where(flag, other, own), jnp.where(flag, own, other)
    gain_grad = jnp.zeros((1, HD), f32)
    for start in range(1024 - BLOCK, -1, -BLOCK):
        rows = slice(start, start + BLOCK)
        length = start + BLOCK
        queries, upstream = q_ref[rows], up_ref[rows]
        scores = masked_scores(
            queries, keys[:length], segc_ref[rows], segr_ref[:, :length], start, length
        )
        probs = jnp.exp(scores - lse_ref[rows])
        value_part = mm_tn(probs.astype(bf16), upstream)
        prob_grad = mm_nt(upstream, values[:length])
        score_grad = (
            probs * (prob_grad - jnp.sum(probs * prob_grad, -1, keepdims=True))
        ).astype(bf16)
        key_part = mm_tn(score_grad, queries)
        if length == 1024:
            value_sum[...] = value_part
            key_sum[...] = key_part
        else:
            value_sum[:length] += value_part
            key_sum[:length] += key_part
        query_grad = mm(score_grad, keys[:length]) * SCALE
        back, part = norm_back(
            raw_ref[rows], gain_ref[...], rotate_back(query_grad, cos_ref[rows], sin_ref[rows])
        )
        low_ref[rows] = back.astype(bf16)
        gain_grad += part
    gain_grad_ref[...] = gain_grad
    key_grad, value_grad = key_sum[...] * SCALE, value_sum[...]
    keep_ref[...] = jnp.where(flag, value_grad, key_grad)
    give_ref[...] = jnp.where(flag, key_grad, value_grad)


def project_back_kernel(
    odd,
    keep_ref,
    got_ref,
    raw_ref,
    gain_ref,
    cos_ref,
    sin_ref,
    low_ref,
    in_ref,
    tokens_ref,
    w_ref,
    half_ref,
    give_ref,
    fold_ref,
    attn_gain_ref,
    gain_grad_ref,
):
    flag = odd[0] == 1
    total = keep_ref[...] + got_ref[...]
    back, part = norm_back(
        raw_ref[...], gain_ref[...], rotate_back(total, cos_ref[...], sin_ref[...])
    )
    gain_grad_ref[...] = jnp.where(flag, 0.0, part)
    raw_grad = jnp.concatenate([low_ref[...], jnp.where(flag, total, back).astype(bf16)], 1)
    attn_gain = jnp.zeros((1, D), f32)
    for start in range(0, 1024, BLOCK):
        rows = slice(start, start + BLOCK)
        blocks = slice(start // 64, (start + BLOCK) // 64)
        in_part = mm_nt(raw_grad[rows], w_ref[...])
        attn_gain += jnp.sum(in_part * rms_norm(tokens_ref[rows].astype(f32)), 0, keepdims=True)
        halves = in_part.reshape(4, 2, 32, D)
        half_ref[blocks] = jnp.where(flag, halves[:, 1], halves[:, 0])
        give_ref[blocks] = jnp.where(flag, halves[:, 0], halves[:, 1]).astype(bf16)
        w_grad = mm_tn(in_ref[:, rows], raw_grad).astype(bf16).reshape(4, 4, 16, 256)
        for i in range(4):
            fold_ref[blocks, :, 256 * i : 256 * i + 256] = w_grad[:, i]
    attn_gain_ref[...] = attn_gain


def mlp_grad_kernel(zero, in_ref, up_ref, cot_ref, act_ref, out_ref):
    for start in range(0, D, BLOCK):
        rows = slice(start, start + BLOCK)
        out_ref[rows, :1536] = mm_tn(in_ref[:, rows], up_ref[...]).astype(bf16)
        out_ref[rows, 1536:] = mm_tn(cot_ref[:, rows], act_ref[...]).astype(bf16)


def rope_tables(seg_row):
    length = seg_row.shape[0]
    starts = jnp.zeros((length,), jnp.int32)
    for doc in range(1, 4):
        before = jnp.sum((seg_row < doc).astype(jnp.int32))
        starts = jnp.where(seg_row == doc, before, starts)
    pos = jnp.arange(length, dtype=jnp.int32) - starts
    half_size = HD // 2
    freq_table = jnp.exp(
        jnp.arange(half_size, dtype=f32) * (-2.0 * math.log(rope_base) / HD)
    )
    angles = pos.astype(f32)[:, None] * freq_table
    cosine, sine = jnp.cos(angles), jnp.sin(angles)
    return jnp.concatenate([cosine, cosine], -1), jnp.concatenate([-sine, sine], -1)


def after(values, *others):
    return lax.optimization_barrier((values,) + others)[0]


def fold(rows):
    count = rows.shape[0]
    parts = rows.reshape(count, 4, 16, 256)
    return jnp.concatenate([parts[:, i] for i in range(4)], -1)


def unfold(rows):
    count = rows.shape[0]
    return jnp.stack([rows[:, :, 256 * i : 256 * i + 256] for i in range(4)], 1).reshape(
        count, 64, 256
    )


def shards(
    tokens,
    cotangent,
    segments,
    w_query,
    w_key,
    w_value,
    w_output,
    w_gate,
    w_up,
    w_down,
    norm_attn,
    norm_mlp,
    norm_query,
    norm_key,
):
    core = lax.axis_index("rep") % 2
    odd = core == 1
    ctx = lax.axis_index("ctx")
    seq_role = ctx // 4

    def pick(values, axis, index):
        return lax.dynamic_index_in_dim(values, index, axis, keepdims=False)

    def by_core(own, other):
        return jnp.where(odd, other, own), jnp.where(odd, own, other)

    def lanes(values, count, size):
        return [
            jnp.where(
                odd,
                values[:, (2 * i + 1) * size : (2 * i + 2) * size],
                values[:, 2 * i * size : (2 * i + 1) * size],
            )
            for i in range(count)
        ]

    halves = tokens.reshape(2, 2, 32, D)
    kept = pick(halves, 1, core)
    got = core_swap(pick(halves, 1, 1 - core))
    quad = jnp.concatenate(by_core(kept, got), 0)
    quad_send = jnp.broadcast_to(quad[:, None], (4, 4, 32, D)).reshape(16, 32, D)
    query_parts = lanes(w_query[0], 4, HD)
    kv_w = jnp.where(odd, w_value[0], w_key[0])
    head_w = jnp.stack(
        [
            jnp.concatenate([query_parts[i], kv_w[:, i * HD : (i + 1) * HD]], 1)
            for i in range(4)
        ]
    )
    head_send = jnp.broadcast_to(fold(head_w)[None], (4, 4, 16, D)).reshape(16, 16, D)
    gain_row = jnp.concatenate([norm_attn[0], norm_mlp[0], norm_query[0], norm_key[0]])
    gain_send = jnp.broadcast_to(jnp.pad(gain_row, (0, D - 144)), (16, 8, D))
    fetched = exchange(jnp.concatenate([quad_send, head_send, gain_send], 1))
    seg_other = core_swap(segments)
    cot_own = cotangent.reshape(128, D)
    cot_both = jnp.concatenate([cot_own, core_swap(cot_own)], 0)

    w_gate, w_up, w_down, w_output, _ = lax.optimization_barrier(
        (w_gate, w_up, w_down, w_output, got)
    )
    out_part = jnp.concatenate(
        [
            jnp.where(
                odd,
                w_output[0, (2 * i + 1) * HD : (2 * i + 2) * HD],
                w_output[0, 2 * i * HD : (2 * i + 1) * HD],
            )
            for i in range(4)
        ],
        0,
    )
    down_part = jnp.where(odd, w_down[0, 768:], w_down[0, :768])
    weights = lax.all_gather(
        jnp.concatenate(
            lanes(w_gate[0], 1, 768) + lanes(w_up[0], 1, 768) + [down_part.T, out_part.T], 1
        ),
        "ctx",
        axis=0,
        tiled=True,
    )
    gateup_w = weights[:, :1536]
    down_wt = weights[:, 1536:2304]
    out_wt = weights[:, 2304:]

    token_half = fetched[:, :32]
    seq_halves = by_core(token_half, core_swap(token_half))
    seq_tokens = jnp.stack(seq_halves, 1).reshape(1024, D)
    qkv_w = unfold(fetched[:, 32:48]).reshape(1024, 256)
    gains = fetched[:, 48].astype(f32)
    attn_gain = gains[:, :64].reshape(D)
    mlp_gain = gains[:, 64:128].reshape(D)
    qnorm_gain = gains[:, 128:136].reshape(HD)
    knorm_gain = gains[:, 136:144].reshape(HD)

    seg_pair = jnp.where(seq_role // 2 == core, segments, seg_other)
    seg_row = pick(seg_pair, 0, seq_role % 2)
    cosine, sine = rope_tables(seg_row)
    seg_column, seg_row = seg_row[:, None], seg_row[None, :]
    flag = core.reshape(1)

    def rope(values):
        turned = jnp.concatenate([values[:, HD // 2 :], values[:, : HD // 2]], -1)
        return values * cosine + turned * sine

    attn_in = (rms_norm(seq_tokens.astype(f32)) * attn_gain).astype(bf16)
    raw = mm(attn_in, qkv_w)
    query_raw, kv_raw = raw[:, :HD], raw[:, HD:]
    queries = rope(rms_norm(query_raw) * qnorm_gain).astype(bf16)
    kv_own = jnp.where(odd, kv_raw, rope(rms_norm(kv_raw) * knorm_gain)).astype(bf16)
    kv_other = core_swap(kv_own)
    mixed_head, lse = kernel_call(
        attend_kernel,
        [shape((1024, HD), bf16), shape((1024, 1), f32)],
        4 * 640 * 1024 * HD,
        flag,
        queries,
        kv_own,
        kv_other,
        seg_column,
        seg_row,
    )
    mixed = exchange(after(mixed_head, cot_both).reshape(16, 64, HD)).reshape(4, 4, 64, HD)
    mixed = jnp.concatenate([mixed[:, i] for i in range(4)], -1).reshape(256, 512)

    def pair_sum(own, other):
        part = (own + core_swap(other.astype(bf16)).astype(f32)).astype(bf16)
        return part.astype(f32) + tp_swap(part).astype(f32)

    mixed_out = mm_nt(mixed, out_wt).reshape(2, 128, D)
    hidden = tokens.reshape(128, D).astype(f32)
    hidden_mid = hidden + pair_sum(pick(mixed_out, 0, core), pick(mixed_out, 0, 1 - core))

    mlp_own = (rms_norm(hidden_mid) * mlp_gain).astype(bf16)
    mlp_in = jnp.concatenate([mlp_own, core_swap(mlp_own)], 0)
    gate_up = mm(mlp_in, gateup_w)
    gate_pre, up_pre = gate_up[:, :768], gate_up[:, 768:]
    sig = jax.nn.sigmoid(gate_pre)
    act = (gate_pre * sig * up_pre).astype(bf16)
    act_grad = mm(cot_both, down_wt)
    gate_grad = (act_grad * up_pre * sig * (1.0 + gate_pre * (1.0 - sig))).astype(bf16)
    up_grad = (act_grad * (gate_pre * sig)).astype(bf16)
    gateup_grad = jnp.concatenate([gate_grad, up_grad], 1)
    mlp_back = mm_nt(gateup_grad, gateup_w)
    mlp_in_grad = pair_sum(mlp_back[:128], mlp_back[128:])
    mlp_w_grad = kernel_call(
        mlp_grad_kernel,
        [shape((D, 2304), bf16)],
        2 * 256 * 2304 * D,
        flag,
        mlp_in,
        gateup_grad,
        cot_both,
        act,
    )[0]
    mlp_w_grad = lax.psum_scatter(mlp_w_grad, "ctx", scatter_dimension=0, tiled=True)
    mid_back, mlp_gain_grad = norm_back(hidden_mid, mlp_gain, mlp_in_grad)
    grad = cot_own.astype(f32) + mid_back
    grad_own = grad.astype(bf16)
    grad_low = jnp.concatenate(by_core(grad_own, core_swap(grad_own)), 0)
    mixed_grad = mm(grad_low, out_wt).astype(bf16)
    mixed_grad = jnp.concatenate(
        [
            mixed_grad[64 * i : 64 * i + 64, HD * j : HD * j + HD]
            for i in range(4)
            for j in range(4)
        ],
        0,
    )
    mixed_grad = exchange(mixed_grad.reshape(16, 64, HD)).reshape(1024, HD)
    mlp_out = mm_nt(after(act, mixed_grad), down_wt)
    out_tokens = hidden_mid + pair_sum(mlp_out[:128], mlp_out[128:])
    out_w_grad = mm_tn(after(grad_low, mixed_grad), mixed).astype(bf16)
    out_w_grad = jnp.sum(exchange(out_w_grad.reshape(16, 64, 512)).astype(f32), 0).astype(bf16)

    kv_keep, kv_give, query_low, qgain_grad = kernel_call_scratch(
        attend_back_kernel,
        [
            shape((1024, HD), f32),
            shape((1024, HD), f32),
            shape((1024, HD), bf16),
            shape((1, HD), f32),
        ],
        [pltpu.VMEM((1024, HD), f32), pltpu.VMEM((1024, HD), f32)],
        10 * 640 * 1024 * HD,
        flag,
        queries,
        kv_own,
        kv_other,
        seg_column,
        seg_row,
        lse,
        mixed_grad,
        query_raw,
        qnorm_gain[None],
        cosine,
        sine,
    )
    in_half, in_give, qkv_fold, attn_gain_grad, kgain_grad = kernel_call(
        project_back_kernel,
        [
            shape((16, 32, D), f32),
            shape((16, 32, D), bf16),
            shape((16, 16, D), bf16),
            shape((1, D), f32),
            shape((1, HD), f32),
        ],
        4 * 1024 * 1024 * 256,
        flag,
        kv_keep,
        core_swap(kv_give),
        kv_raw,
        knorm_gain[None],
        cosine,
        sine,
        query_low,
        attn_in,
        seq_tokens,
        qkv_w,
    )
    in_pair = in_half + core_swap(in_give).astype(f32)
    gain_grads = jnp.concatenate(
        [
            attn_gain_grad.reshape(16, 64),
            (0.5 * mlp_gain_grad).reshape(16, 64),
            qgain_grad.reshape(16, 8),
            kgain_grad.reshape(16, 8),
        ],
        1,
    ).astype(bf16)
    gain_grads = jnp.pad(gain_grads[:, None], ((0, 0), (0, 7), (0, D - 144)))
    returned = exchange(
        after(
            jnp.concatenate([in_pair.astype(bf16), qkv_fold, gain_grads], 1),
            out_tokens,
            out_w_grad,
        )
    )
    in_sum = jnp.sum(returned[:, :32].reshape(4, 4, 32, D).astype(f32), 1).reshape(128, D)
    gain_sum = jnp.sum(returned[:, 48:].astype(f32), 0)
    in_sum = jnp.concatenate([in_sum, gain_sum, jnp.zeros((8, D), f32)], 0).astype(bf16)
    in_sum = in_sum.astype(f32) + tp_swap(in_sum).astype(f32)
    gain_sum = in_sum[128, :256]
    in_sum = in_sum[:128].reshape(2, 2, 32, D)
    in_own = by_core(pick(in_sum, 0, core), core_swap(pick(in_sum, 0, 1 - core)))
    attn_in_grad = jnp.stack(in_own, 1).reshape(128, D)
    input_back, _ = norm_back(hidden, attn_gain, attn_in_grad)
    tokens_grad = grad + input_back

    def owned(part):
        return part.astype(f32) + zlo_swap(part).astype(f32)

    def both(part):
        return by_core(part, core_swap(part))

    mlp_grads = both(owned(mlp_w_grad))
    out_grads = both(owned(out_w_grad))
    qkv_sum = jnp.sum(unfold(returned[:, 32:48]).reshape(4, 4, 64, 256).astype(f32), 0)
    qkv_grads = both(owned(qkv_sum.astype(bf16)))
    gain_sum = gain_sum + zlo_swap(gain_sum)
    gain_sum = gain_sum + core_swap(gain_sum)

    even_qkv, odd_qkv = qkv_grads
    query_w_grad = [part[i, :, :HD] for i in range(4) for part in qkv_grads]
    out_w_grad = [part.T[i * HD : (i + 1) * HD] for i in range(4) for part in out_grads]
    return (
        out_tokens.reshape(2, 64, D),
        tokens_grad.reshape(2, 64, D),
        jnp.concatenate(query_w_grad, 1)[None],
        jnp.concatenate([even_qkv[i, :, HD:] for i in range(4)], 1)[None],
        jnp.concatenate([odd_qkv[i, :, HD:] for i in range(4)], 1)[None],
        jnp.concatenate(out_w_grad, 0)[None],
        jnp.concatenate([part[:, :768] for part in mlp_grads], 1)[None],
        jnp.concatenate([part[:, 768:1536] for part in mlp_grads], 1)[None],
        jnp.concatenate([part[:, 1536:].T for part in mlp_grads], 0)[None],
        gain_sum[None, :64],
        gain_sum[None, 64:128],
        gain_sum[None, 128:136],
        gain_sum[None, 136:144],
    )


def solution(mesh):
    rows = P(None, "ctx", "tp")
    columns = P(None, "tp", "ctx")
    gain = P(None, "ctx")
    token = P("rep", "ctx", None)
    weight_specs = (rows, rows, rows, columns, rows, rows, columns, gain, gain, gain, gain)
    return jax.shard_map(
        shards,
        mesh=mesh,
        in_specs=(token, token, P("rep", None)) + weight_specs,
        out_specs=(token, token) + weight_specs,
        check_vma=False,
    )
```

profile of v0, /device:TPU:1, one launch (start us, length us, event | category | flops | bytes accessed | tf_op | source)
XLA Modules:
  0.0 276.8 jit_solution(6482483570570342956)
XLA Ops:
  16.6 7.0 %all-to-all-start = ((bf16[16,56,1024]{2,1,0:T(8,128)(2,1)}), bf16[16,56,1024]{2,1,0:T(8,128)(2,1)S(1)}, u32[]{:S(2)}, u32[]{:S(2)}) async-start(bf16[16,56,1024]{2,1,0:T(8,128)(2,1)} %pad_maximum_fusion.1), calls=%async_computation | async-start | bytes 3670016 | tf_op jit(solution)/shard_map/all_to_all | solution.py:33
  26.0 2.0 compare_select_fusion.2
  28.0 3.1 %fusion.61 = (f32[1024,64]{1,0:T(8,128)}, f32[1024,64]{1,0:T(8,128)}, f32[1024,64]{1,0:T(8,128)}) fusion(f32[64]{0:T(128)S(1)} %multiply_exponential_fusion, f32[1024]{0:T(1024)S(1)} %subtract_convert_fusion), kind=kLoop, calls=%fused_computation.134 | loop fusion | flops 131072 | bytes 790784 | tf_op jit(solution)/shard_map/neg | solution.py:235
  31.2 22.7 %all-to-all-done = bf16[16,56,1024]{2,1,0:T(8,128)(2,1)S(1)} async-done(((bf16[16,56,1024]{2,1,0:T(8,128)(2,1)}), bf16[16,56,1024]{2,1,0:T(8,128)(2,1)S(1)}, u32[]{:S(2)}, u32[]{:S(2)}) %all-to-all-start) | async-done | bytes 1835040 | tf_op jit(solution)/shard_map/all_to_all | solution.py:33
  55.0 3.3 %collective-permute-start.1 = (bf16[16,32,1024]{2,1,0:T(8,128)(2,1)}, bf16[16,32,1024]{2,1,0:T(8,128)(2,1)}, u32[]{:S(2)}, u32[]{:S(2)}) collective-permute-start(bf16[16,32,1024]{2,1,0:T(8,128)(2,1)} %slice.496), channel_id=1, source_target_pairs={{0,32},{32,0},{64,96},{96,64},{1,33},{33,1},{65,97},{97,65},{2,34}... | collective-permute-start | bytes 3145736 | tf_op jit(solution)/shard_map/ppermute | solution.py:21
  68.9 2.3 shard_map.237
  71.9 13.0 %all_to_all.25 = bf16[16,64,128]{2,1,0:T(8,128)(2,1)S(1)} all-to-all(bf16[16,64,128]{2,1,0:T(8,128)(2,1)S(1)} %bitcast.244), channel_id=1, replica_groups=mesh['rep'=4,'ctx'=16,'tp'=2] {'ctx'}, dimensions={0} | all-to-all | bytes 524288 | tf_op jit(solution)/shard_map/all_to_all | solution.py:33
  85.6 9.1 %all-gather.2.cloned.1.call-done = bf16[1024,2816]{1,0:T(8,128)(2,1)} async-done(((bf16[64,2816]{1,0:T(8,128)(2,1)}), bf16[1024,2816]{1,0:T(8,128)(2,1)}) %all-gather.2.cloned.1.call-update) | async-done | bytes 5767184 | tf_op jit(solution)/shard_map/all_gather | solution.py:328
  94.7 1.8 fusion.11
  98.6 2.9 %collective-permute-start.6 = (bf16[128,1024]{1,0:T(8,128)(2,1)S(1)}, bf16[128,1024]{1,0:T(8,128)(2,1)}, u32[]{:S(2)}, u32[]{:S(2)}) collective-permute-start(bf16[128,1024]{1,0:T(8,128)(2,1)S(1)} %fusion.31), channel_id=1, source_target_pairs={{0,1},{1,0},{2,3},{3,2},{4,5},{5,4},{6,7},{7,6},{8,9},{9,8},{10,11... | collective-permute-start | bytes 786440 | tf_op jit(solution)/shard_map/ppermute | solution.py:29
  101.6 6.2 %collective-permute-done.6 = bf16[128,1024]{1,0:T(8,128)(2,1)} collective-permute-done((bf16[128,1024]{1,0:T(8,128)(2,1)S(1)}, bf16[128,1024]{1,0:T(8,128)(2,1)}, u32[]{:S(2)}, u32[]{:S(2)}) %collective-permute-start.6) | collective-permute-done | bytes 262176 | tf_op jit(solution)/shard_map/ppermute | solution.py:29
  111.8 3.0 %fusion.5 = f32[256,1536]{1,0:T(8,128)S(1)} fusion(bf16[1024,2816]{1,0:T(8,128)(2,1)} %all-gather.2.cloned.1.call-done, bf16[128,1024]{1,0:T(8,128)(2,1)S(1)} %collective-permute-done.7, bf16[128,1024]{1,0:T(8,128)(2,1)S(1)} %multiply_convert_fusion.4), kind=kOutput, calls=%fused_computation.8 | convolution fusion | flops 806354944 | bytes 5242880 | tf_op jit(solution)/shard_map/dot_general | solution.py:37
  119.3 2.9 %collective-permute-start.9 = (bf16[128,1024]{1,0:T(8,128)(2,1)S(1)}, bf16[128,1024]{1,0:T(8,128)(2,1)}, u32[]{:S(2)}, u32[]{:S(2)}) collective-permute-start(bf16[128,1024]{1,0:T(8,128)(2,1)S(1)} %fusion.22), channel_id=1, source_target_pairs={{0,1},{1,0},{2,3},{3,2},{4,5},{5,4},{6,7},{7,6},{8,9},{9,8},{10,11... | collective-permute-start | bytes 786440 | tf_op jit(solution)/shard_map/ppermute | solution.py:29
  125.6 2.9 %collective-permute-done.9 = bf16[128,1024]{1,0:T(8,128)(2,1)} collective-permute-done((bf16[128,1024]{1,0:T(8,128)(2,1)S(1)}, bf16[128,1024]{1,0:T(8,128)(2,1)}, u32[]{:S(2)}, u32[]{:S(2)}) %collective-permute-start.9) | collective-permute-done | bytes 262176 | tf_op jit(solution)/shard_map/ppermute | solution.py:29
  132.8 1.9 multiply_convert_fusion.in_ref
  138.2 5.0 %all-to-all-start.2 = ((bf16[16,64,128]{2,1,0:T(8,128)(2,1)}), bf16[16,64,128]{2,1,0:T(8,128)(2,1)}, u32[]{:S(2)}, u32[]{:S(2)}) async-start(bf16[16,64,128]{2,1,0:T(8,128)(2,1)} %bitcast.264), calls=%async_computation.2 | async-start | bytes 524288 | tf_op jit(solution)/shard_map/all_to_all | solution.py:33
  146.4 3.6 %shard_map.240 = bf16[1024,2304]{1,0:T(8,128)(2,1)} custom-call(s32[1]{0:T(128)} %bitcast.1.odd.zero, bf16[256,1024]{1,0:T(8,128)(2,1)S(1)} %pad_maximum_fusion.8.in_ref, bf16[256,1536]{1,0:T(8,128)(2,1)S(1)} %pad_maximum_fusion.3.up_ref, bf16[256,1024]{1,0:T(8,128)(2,1)S(1)} %copy-done.2, bf16[256,768]{1,0:T(8,128)(2,1)S(1)} %copy-done.3), custom_call_target="tpu_custom_call" | custom-call | flops 1207959552 | bytes 6946820 | tf_op jit(solution)/shard_map/pallas_call | solution.py:76
  151.9 2.1 fusion.7
  157.2 6.4 %all-to-all-start.3 = ((bf16[16,64,512]{2,1,0:T(8,128)(2,1)}), bf16[16,64,512]{2,1,0:T(8,128)(2,1)}, u32[]{:S(2)}, u32[]{:S(2)}) async-start(bf16[16,64,512]{2,1,0:T(8,128)(2,1)} %bitcast.260), calls=%async_computation.3 | async-start | bytes 2097152 | tf_op jit(solution)/shard_map/all_to_all | solution.py:33
  165.7 4.9 %shard_map.238 = (f32[1024,128]{1,0:T(8,128)S(1)}, f32[1024,128]{1,0:T(8,128)}, bf16[1024,128]{1,0:T(8,128)(2,1)S(1)}, f32[1,128]{1,0:T(1,128)S(1)}) custom-call(s32[1]{0:T(128)} %bitcast.1.odd.zero, bf16[1024,128]{1,0:T(8,128)(2,1)S(1)} %get-tuple-element.93.q_ref, bf16[1024,128]{1,0:T(8,128)(2,1)S(1)} %get-tuple-element.60.own_ref, ...), custom_call_target="tpu_custom_call" | custom-call | flops 838860800 | bytes 3945476 | tf_op jit(solution)/shard_map/pallas_call | solution.py:76
  173.7 3.2 %collective-permute-start.12 = (bf16[128,1024]{1,0:T(8,128)(2,1)S(1)}, bf16[128,1024]{1,0:T(8,128)(2,1)}, u32[]{:S(2)}, u32[]{:S(2)}) collective-permute-start(bf16[128,1024]{1,0:T(8,128)(2,1)S(1)} %fusion.21), channel_id=1, source_target_pairs={{0,1},{1,0},{2,3},{3,2},{4,5},{5,4},{6,7},{7,6},{8,9},{9,8},{10,11... | collective-permute-start | bytes 786440 | tf_op jit(solution)/shard_map/ppermute | solution.py:29
  179.2 7.5 %shard_map.239 = (f32[16,32,1024]{2,1,0:T(8,128)}, bf16[16,32,1024]{2,1,0:T(8,128)(2,1)}, bf16[16,16,1024]{2,1,0:T(8,128)(2,1)S(1)}, f32[1,1024]{1,0:T(1,128)S(1)}, f32[1,128]{1,0:T(1,128)S(1)}) custom-call(s32[1]{0:T(128)} %bitcast.1.odd.zero, f32[1024,128]{1,0:T(8,128)S(1)} %copy-done.10, f32[1024,128]{1,0:T(8,128)S(1)} %collective-permute-done.13.got_ref, ...), custom_call_target="tpu_custom_call" | custom-call | flops 1073741824 | bytes 11277316 | tf_op jit(solution)/shard_map/pallas_call | solution.py:76
  186.9 1.8 add_add_fusion
  190.7 3.2 %collective-permute-done.19 = bf16[64,512]{1,0:T(8,128)(2,1)S(1)} collective-permute-done((bf16[64,512]{1,0:T(8,128)(2,1)S(1)}, bf16[64,512]{1,0:T(8,128)(2,1)S(1)}, u32[]{:S(2)}, u32[]{:S(2)}) %collective-permute-start.19) | collective-permute-done | bytes 65568 | tf_op jit(solution)/shard_map/ppermute | solution.py:25
  195.9 2.0 add_convert_fusion
  199.3 7.0 %all-to-all-start.4 = ((bf16[16,56,1024]{2,1,0:T(8,128)(2,1)}), bf16[16,56,1024]{2,1,0:T(8,128)(2,1)S(1)}, u32[]{:S(2)}, u32[]{:S(2)}) async-start(bf16[16,56,1024]{2,1,0:T(8,128)(2,1)} %pad_maximum_fusion.2), calls=%async_computation.4 | async-start | bytes 3670016 | tf_op jit(solution)/shard_map/all_to_all | solution.py:33
  206.4 27.6 %all-to-all-done.4 = bf16[16,56,1024]{2,1,0:T(8,128)(2,1)S(1)} async-done(((bf16[16,56,1024]{2,1,0:T(8,128)(2,1)}), bf16[16,56,1024]{2,1,0:T(8,128)(2,1)S(1)}, u32[]{:S(2)}, u32[]{:S(2)}) %all-to-all-start.4) | async-done | bytes 1835040 | tf_op jit(solution)/shard_map/all_to_all | solution.py:33
  236.5 5.8 %collective-permute-done.15 = bf16[144,1024]{1,0:T(8,128)(2,1)S(1)} collective-permute-done((bf16[144,1024]{1,0:T(8,128)(2,1)S(1)}, bf16[144,1024]{1,0:T(8,128)(2,1)S(1)}, u32[]{:S(2)}, u32[]{:S(2)}) %collective-permute-start.15) | collective-permute-done | bytes 294944 | tf_op jit(solution)/shard_map/ppermute | solution.py:29
  244.0 4.1 %collective-permute-start.18 = (f32[4,64,256]{2,1,0:T(8,128)S(1)}, f32[4,64,256]{2,1,0:T(8,128)S(1)}, u32[]{:S(2)}, u32[]{:S(2)}) collective-permute-start(f32[4,64,256]{2,1,0:T(8,128)S(1)} %convert_add_fusion.3), channel_id=1, source_target_pairs={{0,32},{32,0},{64,96},{96,64},{1,33},{33,1},{65,97},{97,65},{2,34}... | collective-permute-start | bytes 786440 | tf_op jit(solution)/shard_map/ppermute | solution.py:21
  248.1 2.6 collective-permute-start.24
  255.1 7.7 %collective-permute-done.21 = bf16[64,2304]{1,0:T(8,128)(2,1)S(1)} collective-permute-done((bf16[64,2304]{1,0:T(8,128)(2,1)}, bf16[64,2304]{1,0:T(8,128)(2,1)S(1)}, u32[]{:S(2)}, u32[]{:S(2)}) %collective-permute-start.21) | collective-permute-done | bytes 294944 | tf_op jit(solution)/shard_map/ppermute | solution.py:25
  265.3 2.1 fusion.30
  (354 shorter events, 80.3 us)
Async XLA Ops:
  7.3 87.4 %all-gather.2.cloned.1.call-start = ((), (), s32[]{:S(2)}) async-start(), calls=%async_computation.6 | async-start | bytes 6127616 | tf_op jit(solution)/shard_map/all_gather | solution.py:328
  8.3 2.5 collective-permute-start
  16.6 37.3 %all-to-all-start = ((bf16[16,56,1024]{2,1,0:T(8,128)(2,1)}), bf16[16,56,1024]{2,1,0:T(8,128)(2,1)S(1)}, u32[]{:S(2)}, u32[]{:S(2)}) async-start(bf16[16,56,1024]{2,1,0:T(8,128)(2,1)} %pad_maximum_fusion.1), calls=%async_computation | async-start | bytes 3670016 | tf_op jit(solution)/shard_map/all_to_all | solution.py:33
  23.6 1.6 collective-permute-start.2
  24.3 34.0 %collective-permute-start.4 = (bf16[128,1024]{1,0:T(8,128)(2,1)S(1)}, bf16[128,1024]{1,0:T(8,128)(2,1)S(1)}, u32[]{:S(2)}, u32[]{:S(2)}) collective-permute-start(bf16[128,1024]{1,0:T(8,128)(2,1)S(1)} %bitcast.250), channel_id=1, source_target_pairs={{0,32},{32,0},{64,96},{96,64},{1,33},{33,1},{65,97},{97,65},{2,34}... | collective-permute-start | bytes 786440 | tf_op jit(solution)/shard_map/ppermute | solution.py:21
  55.0 6.0 %collective-permute-start.1 = (bf16[16,32,1024]{2,1,0:T(8,128)(2,1)}, bf16[16,32,1024]{2,1,0:T(8,128)(2,1)}, u32[]{:S(2)}, u32[]{:S(2)}) collective-permute-start(bf16[16,32,1024]{2,1,0:T(8,128)(2,1)} %slice.496), channel_id=1, source_target_pairs={{0,32},{32,0},{64,96},{96,64},{1,33},{33,1},{65,97},{97,65},{2,34}... | collective-permute-start | bytes 3145736 | tf_op jit(solution)/shard_map/ppermute | solution.py:21
  59.4 73.4 %copy-start.50 = (f32[1024]{0:T(1024)}, f32[1024]{0:T(1024)S(1)}, u32[]{:S(2)}) copy-start(f32[1024]{0:T(1024)S(1)} %mul.265) | copy-start | bytes 12292
  67.3 1.6 collective-permute-start.3
  96.6 1.9 collective-permute-start.5
  98.6 9.2 %collective-permute-start.6 = (bf16[128,1024]{1,0:T(8,128)(2,1)S(1)}, bf16[128,1024]{1,0:T(8,128)(2,1)}, u32[]{:S(2)}, u32[]{:S(2)}) collective-permute-start(bf16[128,1024]{1,0:T(8,128)(2,1)S(1)} %fusion.31), channel_id=1, source_target_pairs={{0,1},{1,0},{2,3},{3,2},{4,5},{5,4},{6,7},{7,6},{8,9},{9,8},{10,11... | collective-permute-start | bytes 786440 | tf_op jit(solution)/shard_map/ppermute | solution.py:29
  109.2 2.6 collective-permute-start.7
  117.5 1.7 collective-permute-start.8
  119.3 9.2 %collective-permute-start.9 = (bf16[128,1024]{1,0:T(8,128)(2,1)S(1)}, bf16[128,1024]{1,0:T(8,128)(2,1)}, u32[]{:S(2)}, u32[]{:S(2)}) collective-permute-start(bf16[128,1024]{1,0:T(8,128)(2,1)S(1)} %fusion.22), channel_id=1, source_target_pairs={{0,1},{1,0},{2,3},{3,2},{4,5},{5,4},{6,7},{7,6},{8,9},{9,8},{10,11... | collective-permute-start | bytes 786440 | tf_op jit(solution)/shard_map/ppermute | solution.py:29
  131.6 3.3 %collective-permute-start.10 = (bf16[128,1024]{1,0:T(8,128)(2,1)S(1)}, bf16[128,1024]{1,0:T(8,128)(2,1)S(1)}, u32[]{:S(2)}, u32[]{:S(2)}) collective-permute-start(bf16[128,1024]{1,0:T(8,128)(2,1)S(1)} %fusion.74), channel_id=1, source_target_pairs={{0,32},{32,0},{64,96},{96,64},{1,33},{33,1},{65,97},{97,65},{2,34}... | collective-permute-start | bytes 786440 | tf_op jit(solution)/shard_map/ppermute | solution.py:21
  138.2 13.7 %all-to-all-start.2 = ((bf16[16,64,128]{2,1,0:T(8,128)(2,1)}), bf16[16,64,128]{2,1,0:T(8,128)(2,1)}, u32[]{:S(2)}, u32[]{:S(2)}) async-start(bf16[16,64,128]{2,1,0:T(8,128)(2,1)} %bitcast.264), calls=%async_computation.2 | async-start | bytes 524288 | tf_op jit(solution)/shard_map/all_to_all | solution.py:33
  143.2 111.1 %reduce-scatter.2.cloned.1.call-start = ((), (), s32[]{:S(2)}) async-start(), calls=%async_computation.7 | async-start | bytes 5013504 | tf_op jit(solution)/shard_map/reduce_scatter | solution.py:410
  154.8 17.9 %collective-permute-start.11 = (bf16[128,1024]{1,0:T(8,128)(2,1)}, bf16[128,1024]{1,0:T(8,128)(2,1)}, u32[]{:S(2)}, u32[]{:S(2)}) collective-permute-start(bf16[128,1024]{1,0:T(8,128)(2,1)} %slice.719), channel_id=1, source_target_pairs={{0,32},{32,0},{64,96},{96,64},{1,33},{33,1},{65,97},{97,65},{2,34}... | collective-permute-start | bytes 786440 | tf_op jit(solution)/shard_map/ppermute | solution.py:21
  157.2 31.6 %all-to-all-start.3 = ((bf16[16,64,512]{2,1,0:T(8,128)(2,1)}), bf16[16,64,512]{2,1,0:T(8,128)(2,1)}, u32[]{:S(2)}, u32[]{:S(2)}) async-start(bf16[16,64,512]{2,1,0:T(8,128)(2,1)} %bitcast.260), calls=%async_computation.3 | async-start | bytes 2097152 | tf_op jit(solution)/shard_map/all_to_all | solution.py:33
  172.2 4.9 %collective-permute-start.13 = (f32[1024,128]{1,0:T(8,128)}, f32[1024,128]{1,0:T(8,128)S(1)}, u32[]{:S(2)}, u32[]{:S(2)}) collective-permute-start(f32[1024,128]{1,0:T(8,128)} %get-tuple-element.41), channel_id=1, source_target_pairs={{0,32},{32,0},{64,96},{96,64},{1,33},{33,1},{65,97},{97,65},{2,34}... | collective-permute-start | bytes 1572872 | tf_op jit(solution)/shard_map/ppermute | solution.py:21
  173.7 13.2 %collective-permute-start.12 = (bf16[128,1024]{1,0:T(8,128)(2,1)S(1)}, bf16[128,1024]{1,0:T(8,128)(2,1)}, u32[]{:S(2)}, u32[]{:S(2)}) collective-permute-start(bf16[128,1024]{1,0:T(8,128)(2,1)S(1)} %fusion.21), channel_id=1, source_target_pairs={{0,1},{1,0},{2,3},{3,2},{4,5},{5,4},{6,7},{7,6},{8,9},{9,8},{10,11... | collective-permute-start | bytes 786440 | tf_op jit(solution)/shard_map/ppermute | solution.py:29
  186.6 9.3 %collective-permute-start.14 = (bf16[16,32,1024]{2,1,0:T(8,128)(2,1)}, bf16[16,32,1024]{2,1,0:T(8,128)(2,1)S(1)}, u32[]{:S(2)}, u32[]{:S(2)}) collective-permute-start(bf16[16,32,1024]{2,1,0:T(8,128)(2,1)} %get-tuple-element.44), channel_id=1, source_target_pairs={{0,32},{32,0},{64,96},{96,64},{1,33},{33,1},{65,97},{97,65},{2,34}... | collective-permute-start | bytes 3145736 | tf_op jit(solution)/shard_map/ppermute | solution.py:21
  190.2 3.7 %collective-permute-start.19 = (bf16[64,512]{1,0:T(8,128)(2,1)S(1)}, bf16[64,512]{1,0:T(8,128)(2,1)S(1)}, u32[]{:S(2)}, u32[]{:S(2)}) collective-permute-start(bf16[64,512]{1,0:T(8,128)(2,1)S(1)} %reduce_sum.155), channel_id=1, source_target_pairs={{0,64},{32,96},{64,0},{96,32},{1,65},{33,97},{65,1},{97,33},{2,66}... | collective-permute-start | bytes 196616 | tf_op jit(solution)/shard_map/ppermute | solution.py:25
  193.9 1.9 collective-permute-start.20
  199.3 34.8 %all-to-all-start.4 = ((bf16[16,56,1024]{2,1,0:T(8,128)(2,1)}), bf16[16,56,1024]{2,1,0:T(8,128)(2,1)S(1)}, u32[]{:S(2)}, u32[]{:S(2)}) async-start(bf16[16,56,1024]{2,1,0:T(8,128)(2,1)} %pad_maximum_fusion.2), calls=%async_computation.4 | async-start | bytes 3670016 | tf_op jit(solution)/shard_map/all_to_all | solution.py:33
  234.4 7.9 %collective-permute-start.15 = (bf16[144,1024]{1,0:T(8,128)(2,1)S(1)}, bf16[144,1024]{1,0:T(8,128)(2,1)S(1)}, u32[]{:S(2)}, u32[]{:S(2)}) collective-permute-start(bf16[144,1024]{1,0:T(8,128)(2,1)S(1)} %maximum_maximum_fusion), channel_id=1, source_target_pairs={{0,1},{1,0},{2,3},{3,2},{4,5},{5,4},{6,7},{7,6},{8,9},{9,8},{10,11... | collective-permute-start | bytes 884744 | tf_op jit(solution)/shard_map/ppermute | solution.py:29
  235.5 8.5 %collective-permute-start.17 = (bf16[4,64,256]{2,1,0:T(8,128)(2,1)S(1)}, bf16[4,64,256]{2,1,0:T(8,128)(2,1)S(1)}, u32[]{:S(2)}, u32[]{:S(2)}) collective-permute-start(bf16[4,64,256]{2,1,0:T(8,128)(2,1)S(1)} %reduce_sum.159), channel_id=1, source_target_pairs={{0,64},{32,96},{64,0},{96,32},{1,65},{33,97},{65,1},{97,33},{2,66}... | collective-permute-start | bytes 393224 | tf_op jit(solution)/shard_map/ppermute | solution.py:25
  242.5 5.6 %collective-permute-start.23 = (f32[256]{0:T(256)S(1)}, f32[256]{0:T(256)S(1)}, u32[]{:S(2)}, u32[]{:S(2)}) collective-permute-start(f32[256]{0:T(256)S(1)} %bitcast.283), channel_id=1, source_target_pairs={{0,64},{32,96},{64,0},{96,32},{1,65},{33,97},{65,1},{97,33},{2,66}... | collective-permute-start | bytes 3080 | tf_op jit(solution)/shard_map/ppermute | solution.py:25
  244.0 8.7 %collective-permute-start.18 = (f32[4,64,256]{2,1,0:T(8,128)S(1)}, f32[4,64,256]{2,1,0:T(8,128)S(1)}, u32[]{:S(2)}, u32[]{:S(2)}) collective-permute-start(f32[4,64,256]{2,1,0:T(8,128)S(1)} %convert_add_fusion.3), channel_id=1, source_target_pairs={{0,32},{32,0},{64,96},{96,64},{1,33},{33,1},{65,97},{97,65},{2,34}... | collective-permute-start | bytes 786440 | tf_op jit(solution)/shard_map/ppermute | solution.py:21
  248.1 3.4 %collective-permute-start.24 = (f32[256]{0:T(256)S(1)}, f32[256]{0:T(256)S(1)}, u32[]{:S(2)}, u32[]{:S(2)}) collective-permute-start(f32[256]{0:T(256)S(1)} %add.171), channel_id=1, source_target_pairs={{0,32},{32,0},{64,96},{96,64},{1,33},{33,1},{65,97},{97,65},{2,34}... | collective-permute-start | bytes 3080 | tf_op jit(solution)/shard_map/ppermute | solution.py:21
  250.7 3.5 %collective-permute-start.16 = (f32[2,32,1024]{2,1,0:T(8,128)S(1)}, f32[2,32,1024]{2,1,0:T(8,128)S(1)}, u32[]{:S(2)}, u32[]{:S(2)}) collective-permute-start(f32[2,32,1024]{2,1,0:T(8,128)S(1)} %dynamic-slice_bitcast_fusion), channel_id=1, source_target_pairs={{0,32},{32,0},{64,96},{96,64},{1,33},{33,1},{65,97},{97,65},{2,34}... | collective-permute-start | bytes 786440 | tf_op jit(solution)/shard_map/ppermute | solution.py:21
  254.4 8.4 %collective-permute-start.21 = (bf16[64,2304]{1,0:T(8,128)(2,1)}, bf16[64,2304]{1,0:T(8,128)(2,1)S(1)}, u32[]{:S(2)}, u32[]{:S(2)}) collective-permute-start(bf16[64,2304]{1,0:T(8,128)(2,1)} %reduce-scatter.2.cloned.1.call-done), channel_id=1, source_target_pairs={{0,64},{32,96},{64,0},{96,32},{1,65},{33,97},{65,1},{97,33},{2,66}... | collective-permute-start | bytes 884744 | tf_op jit(solution)/shard_map/ppermute | solution.py:25
  263.7 3.8 %collective-permute-start.22 = (f32[64,2304]{1,0:T(8,128)}, f32[64,2304]{1,0:T(8,128)S(1)}, u32[]{:S(2)}, u32[]{:S(2)}) collective-permute-start(f32[64,2304]{1,0:T(8,128)} %convert_add_fusion), channel_id=1, source_target_pairs={{0,32},{32,0},{64,96},{96,64},{1,33},{33,1},{65,97},{97,65},{2,34}... | collective-permute-start | bytes 1769480 | tf_op jit(solution)/shard_map/ppermute | solution.py:21
  (73 other events, 472.2 us)
Sparse Core Ops, SparseCore 0:
  14.6 80.0 all-gather.1
  150.2 102.3 reduce-scatter.1
where the time goes:
time: 278 us; the launch traced here: 277 us
  waiting for transfers between devices  94.2 us (34%)
  starting transfers between devices  59 us (21%)
  other arithmetic  43.2 us (16%)
  local copies, waits for them, and re-layouts  20.3 us (7%)
  Pallas kernels  18.3 us (7%)
  between operations  15.6 us (6%)
  matrix products  13.3 us (5%)
  blocking collectives  13 us (5%)
    all_to_all x4, waiting for transfers between devices, exchange(): return lax.all_to_all(values, 'ctx', 0, 0, tiled=True)  50.4 us
    all_to_all x4, starting transfers between devices, exchange(): return lax.all_to_all(values, 'ctx', 0, 0, tiled=True)  25.4 us
    ppermute x17, starting transfers between devices, core_swap(): return lax.ppermute(values, 'rep', [(0, 1), (1, 0), (2, 3), (3, 2)])  20.8 us
    pallas_call x4, Pallas kernels, kernel_call_scratch(): pl.pallas_call(body, out_shape=out_shape, in_specs=specs, out_specs=[pl.B...  18.3 us
    ppermute x4, waiting for transfers between devices, tp_swap(): return lax.ppermute(values, 'tp', [(0, 1), (1, 0)])  14.9 us
    all_to_all x1, blocking collectives, exchange(): return lax.all_to_all(values, 'ctx', 0, 0, tiled=True)  13 us
    unnamed x178, local copies, waits for them, and re-layouts  11.9 us
    ppermute x4, waiting for transfers between devices, zlo_swap(): return lax.ppermute(values, 'rep', [(0, 2), (1, 3), (2, 0), (3, 1)])  11.7 us
  transfers between devices with their start and end apart: 31, of which 18 were waited for; matrix products, arithmetic and copies ran while one was open for 16% of the time, Pallas kernels for 7%

commit v1 on v0

--- a/solution.py
+++ b/solution.py
@@ -127,8 +127,7 @@
     up_ref,
     raw_ref,
     gain_ref,
-    cos_ref,
-    sin_ref,
+    rope_ref,
     keep_ref,
     give_ref,
     low_ref,
@@ -162,7 +161,9 @@
             key_sum[:length] += key_part
         query_grad = mm(score_grad, keys[:length]) * SCALE
         back, part = norm_back(
-            raw_ref[rows], gain_ref[...], rotate_back(query_grad, cos_ref[rows], sin_ref[rows])
+            raw_ref[rows, :HD],
+            gain_ref[...],
+            rotate_back(query_grad, rope_ref[rows, :HD], rope_ref[rows, HD:]),
         )
         low_ref[rows] = back.astype(bf16)
         gain_grad += part
@@ -178,22 +179,25 @@
     got_ref,
     raw_ref,
     gain_ref,
-    cos_ref,
-    sin_ref,
+    rope_ref,
     low_ref,
-    in_ref,
     tokens_ref,
+    more_tokens_ref,
+    token_gain_ref,
     w_ref,
     half_ref,
     give_ref,
     fold_ref,
     attn_gain_ref,
     gain_grad_ref,
+    attn_in,
 ):
     flag = odd[0] == 1
     total = keep_ref[...] + got_ref[...]
     back, part = norm_back(
-        raw_ref[...], gain_ref[...], rotate_back(total, cos_ref[...], sin_ref[...])
+        raw_ref[:, HD:],
+        gain_ref[...],
+        rotate_back(total, rope_ref[:, :HD], rope_ref[:, HD:]),
     )
     gain_grad_ref[...] = jnp.where(flag, 0.0, part)
     raw_grad = jnp.concatenate([low_ref[...], jnp.where(flag, total, back).astype(bf16)], 1)
@@ -202,21 +206,35 @@
         rows = slice(start, start + BLOCK)
         blocks = slice(start // 64, (start + BLOCK) // 64)
         in_part = mm_nt(raw_grad[rows], w_ref[...])
-        attn_gain += jnp.sum(in_part * rms_norm(tokens_ref[rows].astype(f32)), 0, keepdims=True)
+        held, more = tokens_ref[blocks], more_tokens_ref[blocks]
+        tokens = jnp.stack([jnp.where(flag, more, held), jnp.where(flag, held, more)], 1)
+        normed = rms_norm(tokens.reshape(BLOCK, D).astype(f32))
+        attn_in[rows] = (normed * token_gain_ref[...]).astype(bf16)
+        attn_gain += jnp.sum(in_part * normed, 0, keepdims=True)
         halves = in_part.reshape(4, 2, 32, D)
         half_ref[blocks] = jnp.where(flag, halves[:, 1], halves[:, 0])
         give_ref[blocks] = jnp.where(flag, halves[:, 0], halves[:, 1]).astype(bf16)
-        w_grad = mm_tn(in_ref[:, rows], raw_grad).astype(bf16).reshape(4, 4, 16, 256)
+    for start in range(0, D, BLOCK):
+        rows = slice(start, start + BLOCK)
+        blocks = slice(start // 64, (start + BLOCK) // 64)
+        w_grad = mm_tn(attn_in[:, rows], raw_grad).astype(bf16).reshape(4, 4, 16, 256)
         for i in range(4):
             fold_ref[blocks, :, 256 * i : 256 * i + 256] = w_grad[:, i]
     attn_gain_ref[...] = attn_gain
 
 
-def mlp_grad_kernel(zero, in_ref, up_ref, cot_ref, act_ref, out_ref):
+def mlp_grad_kernel(unused, in_ref, up_ref, cot_ref, act_ref, out_ref):
     for start in range(0, D, BLOCK):
         rows = slice(start, start + BLOCK)
         out_ref[rows, :1536] = mm_tn(in_ref[:, rows], up_ref[...]).astype(bf16)
         out_ref[rows, 1536:] = mm_tn(cot_ref[:, rows], act_ref[...]).astype(bf16)
+
+
+def mixed_grad_kernel(unused, grad_ref, w_ref, out_ref):
+    out = mm(grad_ref[...], w_ref[...]).astype(bf16)
+    for i in range(4):
+        for j in range(4):
+            out_ref[4 * i + j] = out[64 * i : 64 * i + 64, HD * j : HD * j + HD]
 
 
 def rope_tables(seg_row):
@@ -268,8 +286,10 @@
     norm_query,
     norm_key,
 ):
-    core = lax.axis_index("rep") % 2
+    rep = lax.axis_index("rep")
+    core = rep % 2
     odd = core == 1
+    far = rep // 2 == 1
     ctx = lax.axis_index("ctx")
     seq_role = ctx // 4
 
@@ -278,6 +298,9 @@
 
     def by_core(own, other):
         return jnp.where(odd, other, own), jnp.where(odd, own, other)
+
+    def by_far(own, other):
+        return jnp.where(far, other, own), jnp.where(far, own, other)
 
     def lanes(values, count, size):
         return [
@@ -338,7 +361,8 @@
     out_wt = weights[:, 2304:]
 
     token_half = fetched[:, :32]
-    seq_halves = by_core(token_half, core_swap(token_half))
+    more_half = core_swap(token_half)
+    seq_halves = by_core(token_half, more_half)
     seq_tokens = jnp.stack(seq_halves, 1).reshape(1024, D)
     qkv_w = unfold(fetched[:, 32:48]).reshape(1024, 256)
     gains = fetched[:, 48].astype(f32)
@@ -352,6 +376,7 @@
     cosine, sine = rope_tables(seg_row)
     seg_column, seg_row = seg_row[:, None], seg_row[None, :]
     flag = core.reshape(1)
+    rope_both = jnp.concatenate([cosine, sine], 1)
 
     def rope(values):
         turned = jnp.concatenate([values[:, HD // 2 :], values[:, : HD // 2]], -1)
@@ -396,37 +421,31 @@
     up_grad = (act_grad * (gate_pre * sig)).astype(bf16)
     gateup_grad = jnp.concatenate([gate_grad, up_grad], 1)
     mlp_back = mm_nt(gateup_grad, gateup_w)
-    mlp_in_grad = pair_sum(mlp_back[:128], mlp_back[128:])
     mlp_w_grad = kernel_call(
         mlp_grad_kernel,
         [shape((D, 2304), bf16)],
         2 * 256 * 2304 * D,
-        flag,
+        (rep // 2).reshape(1),
         mlp_in,
         gateup_grad,
         cot_both,
         act,
     )[0]
+    mlp_in_grad = after(pair_sum(mlp_back[:128], mlp_back[128:]), mlp_w_grad)
     mlp_w_grad = lax.psum_scatter(mlp_w_grad, "ctx", scatter_dimension=0, tiled=True)
     mid_back, mlp_gain_grad = norm_back(hidden_mid, mlp_gain, mlp_in_grad)
     grad = cot_own.astype(f32) + mid_back
     grad_own = grad.astype(bf16)
     grad_low = jnp.concatenate(by_core(grad_own, core_swap(grad_own)), 0)
-    mixed_grad = mm(grad_low, out_wt).astype(bf16)
-    mixed_grad = jnp.concatenate(
-        [
-            mixed_grad[64 * i : 64 * i + 64, HD * j : HD * j + HD]
-            for i in range(4)
-            for j in range(4)
-        ],
-        0,
-    )
-    mixed_grad = exchange(mixed_grad.reshape(16, 64, HD)).reshape(1024, HD)
-    mlp_out = mm_nt(after(act, mixed_grad), down_wt)
-    out_tokens = hidden_mid + pair_sum(mlp_out[:128], mlp_out[128:])
-    out_w_grad = mm_tn(after(grad_low, mixed_grad), mixed).astype(bf16)
-    out_w_grad = jnp.sum(exchange(out_w_grad.reshape(16, 64, 512)).astype(f32), 0).astype(bf16)
-
+    mixed_grad = kernel_call(
+        mixed_grad_kernel,
+        [shape((16, 64, HD), bf16)],
+        2 * 256 * 512 * D,
+        flag,
+        grad_low,
+        out_wt,
+    )[0]
+    mixed_grad = exchange(mixed_grad).reshape(1024, HD)
     kv_keep, kv_give, query_low, qgain_grad = kernel_call_scratch(
         attend_back_kernel,
         [
@@ -445,12 +464,11 @@
         seg_row,
         lse,
         mixed_grad,
-        query_raw,
+        raw,
         qnorm_gain[None],
-        cosine,
-        sine,
-    )
-    in_half, in_give, qkv_fold, attn_gain_grad, kgain_grad = kernel_call(
+        rope_both,
+    )
+    in_half, in_give, qkv_fold, attn_gain_grad, kgain_grad = kernel_call_scratch(
         project_back_kernel,
         [
             shape((16, 32, D), f32),
@@ -459,17 +477,18 @@
             shape((1, D), f32),
             shape((1, HD), f32),
         ],
+        [pltpu.VMEM((1024, D), bf16)],
         4 * 1024 * 1024 * 256,
         flag,
         kv_keep,
         core_swap(kv_give),
-        kv_raw,
+        raw,
         knorm_gain[None],
-        cosine,
-        sine,
+        rope_both,
         query_low,
-        attn_in,
-        seq_tokens,
+        token_half,
+        more_half,
+        attn_gain[None],
         qkv_w,
     )
     in_pair = in_half + core_swap(in_give).astype(f32)
@@ -483,13 +502,15 @@
         1,
     ).astype(bf16)
     gain_grads = jnp.pad(gain_grads[:, None], ((0, 0), (0, 7), (0, D - 144)))
-    returned = exchange(
-        after(
-            jnp.concatenate([in_pair.astype(bf16), qkv_fold, gain_grads], 1),
-            out_tokens,
-            out_w_grad,
-        )
-    )
+    sending = jnp.concatenate([in_pair.astype(bf16), qkv_fold, gain_grads], 1)
+    returned = exchange(sending)
+    act, grad_low, _ = lax.optimization_barrier((act, grad_low, sending))
+    mlp_out = mm_nt(act, down_wt)
+    out_tokens = hidden_mid + pair_sum(mlp_out[:128], mlp_out[128:])
+    out_w_grad = mm_tn(grad_low, mixed).astype(bf16)
+    out_w_grad = exchange(after(out_w_grad, returned).reshape(16, 64, 512))
+    returned, mlp_w_grad = lax.optimization_barrier((returned, mlp_w_grad))
+    out_w_grad = jnp.sum(out_w_grad.astype(f32), 0).astype(bf16)
     in_sum = jnp.sum(returned[:, :32].reshape(4, 4, 32, D).astype(f32), 1).reshape(128, D)
     gain_sum = jnp.sum(returned[:, 48:].astype(f32), 0)
     in_sum = jnp.concatenate([in_sum, gain_sum, jnp.zeros((8, D), f32)], 0).astype(bf16)

time: 278 us -> 287 us (1.032)
  waiting for transfers between devices: 94.2 us -> 102 us
  local copies, waits for them, and re-layouts: 20.3 us -> 25.6 us
  starting transfers between devices: 59 us -> 55.4 us
    all_to_all x4, waiting for transfers between devices: 50.4 us -> 65.7 us  [exchange(): return lax.all_to_all(values, 'ctx', 0, 0, tiled=True)]
    ppermute x4, waiting for transfers between devices: 14.9 us -> 8.51 us  [tp_swap(): return lax.ppermute(values, 'tp', [(0, 1), (1, 0)])]
    all_to_all x4, starting transfers between devices: 25.4 us -> 20.3 us  [exchange(): return lax.all_to_all(values, 'ctx', 0, 0, tiled=True)]
    ppermute x4, waiting for transfers between devices: 11.7 us -> 16.2 us  [zlo_swap(): return lax.ppermute(values, 'rep', [(0, 2), (1, 3), (2, 0), (3, 1)])]
    all_gather x1, waiting for transfers between devices: 9.09 us -> 4.9 us  [shards(): lax.all_gather(jnp.concatenate(lanes(w_gate[0], 1, 768) + lanes(w_up[0],...]
    dot_general x4 -> x3, matrix products: 6.87 us -> 4.96 us  [mm(): return jnp.dot(left, right, preferred_element_type=f32)]
    pallas_call x4 -> x5, Pallas kernels: 18.3 us -> 18.2 us  [kernel_call_scratch(): pl.pallas_call(body, out_shape=out_shape, in_specs=specs, out_specs=[pl.B...]
    unnamed x178 -> x143, local copies, waits for them, and re-layouts: 11.9 us -> 12 us
  transfers between devices with their start and end apart: 31 -> 31, of which waited for: 18 -> 17; matrix products, arithmetic and copies ran while one was open for 16% -> 18% of each run, Pallas kernels for 7% -> 6%
where the time goes in v1:
time: 287 us; the launch traced here: 285 us
  waiting for transfers between devices  102 us (36%)
  starting transfers between devices  55.4 us (19%)
  other arithmetic  44.5 us (16%)
  local copies, waits for them, and re-layouts  25.6 us (9%)
  Pallas kernels  18.2 us (6%)
  between operations  15.4 us (5%)
  blocking collectives  13.5 us (5%)
  matrix products  11.2 us (4%)
    all_to_all x4, waiting for transfers between devices, exchange(): return lax.all_to_all(values, 'ctx', 0, 0, tiled=True)  65.7 us
    ppermute x17, starting transfers between devices, core_swap(): return lax.ppermute(values, 'rep', [(0, 1), (1, 0), (2, 3), (3, 2)])  22.2 us
    all_to_all x4, starting transfers between devices, exchange(): return lax.all_to_all(values, 'ctx', 0, 0, tiled=True)  20.3 us
    pallas_call x5, Pallas kernels, kernel_call_scratch(): pl.pallas_call(body, out_shape=out_shape, in_specs=specs, out_specs=[pl.B...  18.2 us
    ppermute x4, waiting for transfers between devices, zlo_swap(): return lax.ppermute(values, 'rep', [(0, 2), (1, 3), (2, 0), (3, 1)])  16.2 us
    all_to_all x1, blocking collectives, exchange(): return lax.all_to_all(values, 'ctx', 0, 0, tiled=True)  13.5 us
    unnamed x143, local copies, waits for them, and re-layouts  12 us
    ppermute x4, starting transfers between devices, tp_swap(): return lax.ppermute(values, 'tp', [(0, 1), (1, 0)])  8.95 us
  transfers between devices with their start and end apart: 31, of which 17 were waited for; matrix products, arithmetic and copies ran while one was open for 18% of the time, Pallas kernels for 6%

profile of v1, /device:TPU:1, one launch (start us, length us, event | category | flops | bytes accessed | tf_op | source)
XLA Modules:
  0.0 285.5 jit_solution(11377038103691282029)
XLA Ops:
  16.6 7.0 %all-to-all-start = ((bf16[16,56,1024]{2,1,0:T(8,128)(2,1)}), bf16[16,56,1024]{2,1,0:T(8,128)(2,1)S(1)}, u32[]{:S(2)}, u32[]{:S(2)}) async-start(bf16[16,56,1024]{2,1,0:T(8,128)(2,1)} %pad_maximum_fusion.1), calls=%async_computation | async-start | bytes 3670016 | tf_op jit(solution)/shard_map/all_to_all | solution.py:33
  28.1 3.1 %fusion.58 = (f32[1024,64]{1,0:T(8,128)}, f32[1024,64]{1,0:T(8,128)}, f32[1024,64]{1,0:T(8,128)}) fusion(f32[64]{0:T(128)S(1)} %multiply_exponential_fusion, f32[1024]{0:T(1024)S(1)} %subtract_convert_fusion), kind=kLoop, calls=%fused_computation.130 | loop fusion | flops 131072 | bytes 790784 | tf_op jit(solution)/shard_map/neg | solution.py:253
  31.2 22.7 %all-to-all-done = bf16[16,56,1024]{2,1,0:T(8,128)(2,1)S(1)} async-done(((bf16[16,56,1024]{2,1,0:T(8,128)(2,1)}), bf16[16,56,1024]{2,1,0:T(8,128)(2,1)S(1)}, u32[]{:S(2)}, u32[]{:S(2)}) %all-to-all-start) | async-done | bytes 1835040 | tf_op jit(solution)/shard_map/all_to_all | solution.py:33
  55.1 3.3 %collective-permute-start.1 = (bf16[16,32,1024]{2,1,0:T(8,128)(2,1)}, bf16[16,32,1024]{2,1,0:T(8,128)(2,1)}, u32[]{:S(2)}, u32[]{:S(2)}) collective-permute-start(bf16[16,32,1024]{2,1,0:T(8,128)(2,1)} %slice.432.tokens_ref), channel_id=1, source_target_pairs={{0,32},{32,0},{64,96},{96,64},{1,33},{33,1},{65,97},{97,65},{2,34}... | collective-permute-start | bytes 3145736 | tf_op jit(solution)/shard_map/ppermute | solution.py:21
  67.6 2.0 fusion.25.own_ref
  70.5 2.1 fusion.22.q_ref
  72.6 2.3 shard_map.237
  75.6 13.5 %all_to_all.25 = bf16[16,64,128]{2,1,0:T(8,128)(2,1)S(1)} all-to-all(bf16[16,64,128]{2,1,0:T(8,128)(2,1)S(1)} %bitcast.240), channel_id=1, replica_groups=mesh['rep'=4,'ctx'=16,'tp'=2] {'ctx'}, dimensions={0} | all-to-all | bytes 524288 | tf_op jit(solution)/shard_map/all_to_all | solution.py:33
  89.8 4.9 %all-gather.2.cloned.1.call-done = bf16[1024,2816]{1,0:T(8,128)(2,1)} async-done(((bf16[64,2816]{1,0:T(8,128)(2,1)}), bf16[1024,2816]{1,0:T(8,128)(2,1)}) %all-gather.2.cloned.1.call-update) | async-done | bytes 5767184 | tf_op jit(solution)/shard_map/all_gather | solution.py:351
  98.6 3.0 %collective-permute-start.6 = (bf16[128,1024]{1,0:T(8,128)(2,1)S(1)}, bf16[128,1024]{1,0:T(8,128)(2,1)}, u32[]{:S(2)}, u32[]{:S(2)}) collective-permute-start(bf16[128,1024]{1,0:T(8,128)(2,1)S(1)} %fusion.29), channel_id=1, source_target_pairs={{0,1},{1,0},{2,3},{3,2},{4,5},{5,4},{6,7},{7,6},{8,9},{9,8},{10,11... | collective-permute-start | bytes 786440 | tf_op jit(solution)/shard_map/ppermute | solution.py:29
  102.3 5.5 %collective-permute-done.6 = bf16[128,1024]{1,0:T(8,128)(2,1)} collective-permute-done((bf16[128,1024]{1,0:T(8,128)(2,1)S(1)}, bf16[128,1024]{1,0:T(8,128)(2,1)}, u32[]{:S(2)}, u32[]{:S(2)}) %collective-permute-start.6) | collective-permute-done | bytes 262176 | tf_op jit(solution)/shard_map/ppermute | solution.py:29
  111.9 3.5 %fusion.5 = f32[256,1536]{1,0:T(8,128)S(1)} fusion(bf16[1024,2816]{1,0:T(8,128)(2,1)} %all-gather.2.cloned.1.call-done, bf16[128,1024]{1,0:T(8,128)(2,1)} %collective-permute-done.7, bf16[128,1024]{1,0:T(8,128)(2,1)S(1)} %multiply_convert_fusion.3), kind=kOutput, calls=%fused_computation.7 | convolution fusion | flops 806354944 | bytes 5242880 | tf_op jit(solution)/shard_map/dot_general | solution.py:37
  119.7 2.9 %collective-permute-start.9 = (bf16[128,1024]{1,0:T(8,128)(2,1)}, bf16[128,1024]{1,0:T(8,128)(2,1)}, u32[]{:S(2)}, u32[]{:S(2)}) collective-permute-start(bf16[128,1024]{1,0:T(8,128)(2,1)} %fusion.20), channel_id=1, source_target_pairs={{0,1},{1,0},{2,3},{3,2},{4,5},{5,4},{6,7},{7,6},{8,9},{9,8},{10,11... | collective-permute-start | bytes 786440 | tf_op jit(solution)/shard_map/ppermute | solution.py:29
  122.5 3.7 %shard_map.238 = bf16[1024,2304]{1,0:T(8,128)(2,1)} custom-call(s32[1]{0:T(128)} %bitcast.50.unused, bf16[256,1024]{1,0:T(8,128)(2,1)S(1)} %pad_maximum_fusion.9.in_ref, bf16[256,1536]{1,0:T(8,128)(2,1)S(1)} %pad_maximum_fusion.4.up_ref, bf16[256,1024]{1,0:T(8,128)(2,1)S(1)} %pad_maximum_fusion.8.cot_ref, bf16[256,768]{1,0:T(8,128)(2,1)S(1)} %get-tuple-element.52.act_ref), custom_call_target="tpu_custom_call" | custom-call | flops 1207959552 | bytes 6946820 | tf_op jit(solution)/shard_map/pallas_call | solution.py:76
  126.2 3.0 %collective-permute-done.9 = bf16[128,1024]{1,0:T(8,128)(2,1)} collective-permute-done((bf16[128,1024]{1,0:T(8,128)(2,1)}, bf16[128,1024]{1,0:T(8,128)(2,1)}, u32[]{:S(2)}, u32[]{:S(2)}) %collective-permute-start.9) | collective-permute-done | bytes 262176 | tf_op jit(solution)/shard_map/ppermute | solution.py:29
  137.0 5.0 %all-to-all-start.2 = ((bf16[16,64,128]{2,1,0:T(8,128)(2,1)}), bf16[16,64,128]{2,1,0:T(8,128)(2,1)}, u32[]{:S(2)}, u32[]{:S(2)}) async-start(bf16[16,64,128]{2,1,0:T(8,128)(2,1)} %shard_map.239), calls=%async_computation.2 | async-start | bytes 524288 | tf_op jit(solution)/shard_map/all_to_all | solution.py:33
  142.0 2.0 pad_maximum_fusion.3.rope_ref
  144.1 6.8 %all-to-all-done.2 = bf16[16,64,128]{2,1,0:T(8,128)(2,1)} async-done(((bf16[16,64,128]{2,1,0:T(8,128)(2,1)}), bf16[16,64,128]{2,1,0:T(8,128)(2,1)}, u32[]{:S(2)}, u32[]{:S(2)}) %all-to-all-start.2) | async-done | bytes 262176 | tf_op jit(solution)/shard_map/all_to_all | solution.py:33
  152.9 4.8 %shard_map.240 = (f32[1024,128]{1,0:T(8,128)S(1)}, f32[1024,128]{1,0:T(8,128)}, bf16[1024,128]{1,0:T(8,128)(2,1)S(1)}, f32[1,128]{1,0:T(1,128)S(1)}) custom-call(s32[1]{0:T(128)} %bitcast.1.odd.unused, bf16[1024,128]{1,0:T(8,128)(2,1)S(1)} %fusion.22.q_ref, bf16[1024,128]{1,0:T(8,128)(2,1)S(1)} %fusion.25.own_ref, bf16[1024,128]{1,0:T(8,128)(2,1)S(1)} %copy-done.5, ...), custom_call_target="tpu_custom_call" | custom-call | flops 838860800 | bytes 4469764 | tf_op jit(solution)/shard_map/pallas_call | solution.py:76
  159.2 2.2 collective-permute-start.11
  166.2 6.4 %shard_map.241 = (f32[16,32,1024]{2,1,0:T(8,128)}, bf16[16,32,1024]{2,1,0:T(8,128)(2,1)}, bf16[16,16,1024]{2,1,0:T(8,128)(2,1)S(1)}, f32[1,1024]{1,0:T(1,128)S(1)}, f32[1,128]{1,0:T(1,128)S(1)}) custom-call(s32[1]{0:T(128)} %bitcast.1.odd.unused, f32[1024,128]{1,0:T(8,128)S(1)} %copy-done.7, f32[1024,128]{1,0:T(8,128)S(1)} %collective-permute-done.11.got_ref, ...), custom_call_target="tpu_custom_call" | custom-call | flops 1073741824 | bytes 9708548 | tf_op jit(solution)/shard_map/pallas_call | solution.py:76
  179.5 3.9 %all-to-all-start.3 = ((bf16[16,56,1024]{2,1,0:T(8,128)(2,1)}), bf16[16,56,1024]{2,1,0:T(8,128)(2,1)S(1)}, u32[]{:S(2)}, u32[]{:S(2)}) async-start(bf16[16,56,1024]{2,1,0:T(8,128)(2,1)} %pad_maximum_fusion.2), calls=%async_computation.3 | async-start | bytes 3670016 | tf_op jit(solution)/shard_map/all_to_all | solution.py:33
  184.8 27.6 %all-to-all-done.3 = bf16[16,56,1024]{2,1,0:T(8,128)(2,1)S(1)} async-done(((bf16[16,56,1024]{2,1,0:T(8,128)(2,1)}), bf16[16,56,1024]{2,1,0:T(8,128)(2,1)S(1)}, u32[]{:S(2)}, u32[]{:S(2)}) %all-to-all-start.3) | async-done | bytes 1835040 | tf_op jit(solution)/shard_map/all_to_all | solution.py:33
  212.4 4.4 %all-to-all-start.4 = ((bf16[16,64,512]{2,1,0:T(8,128)(2,1)}), bf16[16,64,512]{2,1,0:T(8,128)(2,1)}, u32[]{:S(2)}, u32[]{:S(2)}) async-start(bf16[16,64,512]{2,1,0:T(8,128)(2,1)} %bitcast.255), calls=%async_computation.5 | async-start | bytes 2097152 | tf_op jit(solution)/shard_map/all_to_all | solution.py:33
  217.0 2.0 fusion.7
  220.0 2.8 collective-permute-start.13
  222.8 8.6 %all-to-all-done.4 = bf16[16,64,512]{2,1,0:T(8,128)(2,1)} async-done(((bf16[16,64,512]{2,1,0:T(8,128)(2,1)}), bf16[16,64,512]{2,1,0:T(8,128)(2,1)}, u32[]{:S(2)}, u32[]{:S(2)}) %all-to-all-start.4) | async-done | bytes 1048608 | tf_op jit(solution)/shard_map/all_to_all | solution.py:33
  236.0 4.8 %collective-permute-start.20 = (f32[64,512]{1,0:T(8,128)S(1)}, f32[64,512]{1,0:T(8,128)S(1)}, u32[]{:S(2)}, u32[]{:S(2)}) collective-permute-start(f32[64,512]{1,0:T(8,128)S(1)} %convert_add_fusion.4), channel_id=1, source_target_pairs={{0,32},{32,0},{64,96},{96,64},{1,33},{33,1},{65,97},{97,65},{2,34}... | collective-permute-start | bytes 393224 | tf_op jit(solution)/shard_map/ppermute | solution.py:21
  241.9 2.9 %collective-permute-start.14 = (bf16[128,1024]{1,0:T(8,128)(2,1)S(1)}, bf16[128,1024]{1,0:T(8,128)(2,1)}, u32[]{:S(2)}, u32[]{:S(2)}) collective-permute-start(bf16[128,1024]{1,0:T(8,128)(2,1)S(1)} %fusion.14), channel_id=1, source_target_pairs={{0,1},{1,0},{2,3},{3,2},{4,5},{5,4},{6,7},{7,6},{8,9},{9,8},{10,11... | collective-permute-start | bytes 786440 | tf_op jit(solution)/shard_map/ppermute | solution.py:29
  248.6 12.1 %collective-permute-done.17 = bf16[4,64,256]{2,1,0:T(8,128)(2,1)S(1)} collective-permute-done((bf16[4,64,256]{2,1,0:T(8,128)(2,1)S(1)}, bf16[4,64,256]{2,1,0:T(8,128)(2,1)S(1)}, u32[]{:S(2)}, u32[]{:S(2)}) %collective-permute-start.17) | collective-permute-done | bytes 131104 | tf_op jit(solution)/shard_map/ppermute | solution.py:25
  264.8 2.3 collective-permute-done.23
  272.8 2.2 fusion.28
  (319 shorter events, 86.9 us)
Async XLA Ops:
  7.3 87.4 %all-gather.2.cloned.1.call-start = ((), (), s32[]{:S(2)}) async-start(), calls=%async_computation.6 | async-start | bytes 6127616 | tf_op jit(solution)/shard_map/all_gather | solution.py:351
  8.3 2.5 collective-permute-start
  16.6 37.3 %all-to-all-start = ((bf16[16,56,1024]{2,1,0:T(8,128)(2,1)}), bf16[16,56,1024]{2,1,0:T(8,128)(2,1)S(1)}, u32[]{:S(2)}, u32[]{:S(2)}) async-start(bf16[16,56,1024]{2,1,0:T(8,128)(2,1)} %pad_maximum_fusion.1), calls=%async_computation | async-start | bytes 3670016 | tf_op jit(solution)/shard_map/all_to_all | solution.py:33
  23.6 221.4 %reduce-scatter.2.cloned.1.call-start = ((), (), s32[]{:S(2)}) async-start(), calls=%async_computation.7 | async-start | bytes 5013504 | tf_op jit(solution)/shard_map/reduce_scatter | solution.py:435
  23.6 1.6 collective-permute-start.2
  24.4 34.1 %collective-permute-start.4 = (bf16[128,1024]{1,0:T(8,128)(2,1)S(1)}, bf16[128,1024]{1,0:T(8,128)(2,1)S(1)}, u32[]{:S(2)}, u32[]{:S(2)}) collective-permute-start(bf16[128,1024]{1,0:T(8,128)(2,1)S(1)} %bitcast.245), channel_id=1, source_target_pairs={{0,32},{32,0},{64,96},{96,64},{1,33},{33,1},{65,97},{97,65},{2,34}... | collective-permute-start | bytes 786440 | tf_op jit(solution)/shard_map/ppermute | solution.py:21
  55.1 7.9 %collective-permute-start.1 = (bf16[16,32,1024]{2,1,0:T(8,128)(2,1)}, bf16[16,32,1024]{2,1,0:T(8,128)(2,1)}, u32[]{:S(2)}, u32[]{:S(2)}) collective-permute-start(bf16[16,32,1024]{2,1,0:T(8,128)(2,1)} %slice.432.tokens_ref), channel_id=1, source_target_pairs={{0,32},{32,0},{64,96},{96,64},{1,33},{33,1},{65,97},{97,65},{2,34}... | collective-permute-start | bytes 3145736 | tf_op jit(solution)/shard_map/ppermute | solution.py:21
  69.7 2.9 %collective-permute-start.3 = (bf16[1024,128]{1,0:T(8,128)(2,1)S(1)}, bf16[1024,128]{1,0:T(8,128)(2,1)S(1)}, u32[]{:S(2)}, u32[]{:S(2)}) collective-permute-start(bf16[1024,128]{1,0:T(8,128)(2,1)S(1)} %fusion.25.own_ref), channel_id=1, source_target_pairs={{0,32},{32,0},{64,96},{96,64},{1,33},{33,1},{65,97},{97,65},{2,34}... | collective-permute-start | bytes 786440 | tf_op jit(solution)/shard_map/ppermute | solution.py:21
  96.6 1.9 collective-permute-start.5
  98.6 9.2 %collective-permute-start.6 = (bf16[128,1024]{1,0:T(8,128)(2,1)S(1)}, bf16[128,1024]{1,0:T(8,128)(2,1)}, u32[]{:S(2)}, u32[]{:S(2)}) collective-permute-start(bf16[128,1024]{1,0:T(8,128)(2,1)S(1)} %fusion.29), channel_id=1, source_target_pairs={{0,1},{1,0},{2,3},{3,2},{4,5},{5,4},{6,7},{7,6},{8,9},{9,8},{10,11... | collective-permute-start | bytes 786440 | tf_op jit(solution)/shard_map/ppermute | solution.py:29
  109.2 2.8 collective-permute-start.7
  117.3 1.6 collective-permute-start.8
  119.7 9.6 %collective-permute-start.9 = (bf16[128,1024]{1,0:T(8,128)(2,1)}, bf16[128,1024]{1,0:T(8,128)(2,1)}, u32[]{:S(2)}, u32[]{:S(2)}) collective-permute-start(bf16[128,1024]{1,0:T(8,128)(2,1)} %fusion.20), channel_id=1, source_target_pairs={{0,1},{1,0},{2,3},{3,2},{4,5},{5,4},{6,7},{7,6},{8,9},{9,8},{10,11... | collective-permute-start | bytes 786440 | tf_op jit(solution)/shard_map/ppermute | solution.py:29
  132.6 2.4 collective-permute-start.10
  137.0 13.9 %all-to-all-start.2 = ((bf16[16,64,128]{2,1,0:T(8,128)(2,1)}), bf16[16,64,128]{2,1,0:T(8,128)(2,1)}, u32[]{:S(2)}, u32[]{:S(2)}) async-start(bf16[16,64,128]{2,1,0:T(8,128)(2,1)} %shard_map.239), calls=%async_computation.2 | async-start | bytes 524288 | tf_op jit(solution)/shard_map/all_to_all | solution.py:33
  159.2 4.0 %collective-permute-start.11 = (f32[1024,128]{1,0:T(8,128)}, f32[1024,128]{1,0:T(8,128)S(1)}, u32[]{:S(2)}, u32[]{:S(2)}) collective-permute-start(f32[1024,128]{1,0:T(8,128)} %get-tuple-element.44), channel_id=1, source_target_pairs={{0,32},{32,0},{64,96},{96,64},{1,33},{33,1},{65,97},{97,65},{2,34}... | collective-permute-start | bytes 1572872 | tf_op jit(solution)/shard_map/ppermute | solution.py:21
  173.1 2.9 %collective-permute-start.12 = (bf16[16,32,1024]{2,1,0:T(8,128)(2,1)}, bf16[16,32,1024]{2,1,0:T(8,128)(2,1)S(1)}, u32[]{:S(2)}, u32[]{:S(2)}) collective-permute-start(bf16[16,32,1024]{2,1,0:T(8,128)(2,1)} %get-tuple-element.47), channel_id=1, source_target_pairs={{0,32},{32,0},{64,96},{96,64},{1,33},{33,1},{65,97},{97,65},{2,34}... | collective-permute-start | bytes 3145736 | tf_op jit(solution)/shard_map/ppermute | solution.py:21
  179.5 33.0 %all-to-all-start.3 = ((bf16[16,56,1024]{2,1,0:T(8,128)(2,1)}), bf16[16,56,1024]{2,1,0:T(8,128)(2,1)S(1)}, u32[]{:S(2)}, u32[]{:S(2)}) async-start(bf16[16,56,1024]{2,1,0:T(8,128)(2,1)} %pad_maximum_fusion.2), calls=%async_computation.3 | async-start | bytes 3670016 | tf_op jit(solution)/shard_map/all_to_all | solution.py:33
  183.4 33.5 %copy-start.21 = (bf16[2,64,1024]{2,1,0:T(8,128)(2,1)S(1)}, bf16[2,64,1024]{2,1,0:T(8,128)(2,1)}, u32[]{:S(2)}) copy-start(bf16[2,64,1024]{2,1,0:T(8,128)(2,1)} %param.14) | copy-start | bytes 786436
  212.4 19.0 %all-to-all-start.4 = ((bf16[16,64,512]{2,1,0:T(8,128)(2,1)}), bf16[16,64,512]{2,1,0:T(8,128)(2,1)}, u32[]{:S(2)}, u32[]{:S(2)}) async-start(bf16[16,64,512]{2,1,0:T(8,128)(2,1)} %bitcast.255), calls=%async_computation.5 | async-start | bytes 2097152 | tf_op jit(solution)/shard_map/all_to_all | solution.py:33
  220.0 20.8 %collective-permute-start.13 = (bf16[128,1024]{1,0:T(8,128)(2,1)S(1)}, bf16[128,1024]{1,0:T(8,128)(2,1)S(1)}, u32[]{:S(2)}, u32[]{:S(2)}) collective-permute-start(bf16[128,1024]{1,0:T(8,128)(2,1)S(1)} %slice.615), channel_id=1, source_target_pairs={{0,32},{32,0},{64,96},{96,64},{1,33},{33,1},{65,97},{97,65},{2,34}... | collective-permute-start | bytes 786440 | tf_op jit(solution)/shard_map/ppermute | solution.py:21
  232.8 3.2 %collective-permute-start.19 = (bf16[64,512]{1,0:T(8,128)(2,1)S(1)}, bf16[64,512]{1,0:T(8,128)(2,1)S(1)}, u32[]{:S(2)}, u32[]{:S(2)}) collective-permute-start(bf16[64,512]{1,0:T(8,128)(2,1)S(1)} %reduce_sum.159), channel_id=1, source_target_pairs={{0,64},{32,96},{64,0},{96,32},{1,65},{33,97},{65,1},{97,33},{2,66}... | collective-permute-start | bytes 196616 | tf_op jit(solution)/shard_map/ppermute | solution.py:25
  236.0 8.7 %collective-permute-start.20 = (f32[64,512]{1,0:T(8,128)S(1)}, f32[64,512]{1,0:T(8,128)S(1)}, u32[]{:S(2)}, u32[]{:S(2)}) collective-permute-start(f32[64,512]{1,0:T(8,128)S(1)} %convert_add_fusion.4), channel_id=1, source_target_pairs={{0,32},{32,0},{64,96},{96,64},{1,33},{33,1},{65,97},{97,65},{2,34}... | collective-permute-start | bytes 393224 | tf_op jit(solution)/shard_map/ppermute | solution.py:21
  241.9 30.9 %collective-permute-start.14 = (bf16[128,1024]{1,0:T(8,128)(2,1)S(1)}, bf16[128,1024]{1,0:T(8,128)(2,1)}, u32[]{:S(2)}, u32[]{:S(2)}) collective-permute-start(bf16[128,1024]{1,0:T(8,128)(2,1)S(1)} %fusion.14), channel_id=1, source_target_pairs={{0,1},{1,0},{2,3},{3,2},{4,5},{5,4},{6,7},{7,6},{8,9},{9,8},{10,11... | collective-permute-start | bytes 786440 | tf_op jit(solution)/shard_map/ppermute | solution.py:29
  246.0 16.1 %collective-permute-start.15 = (bf16[144,1024]{1,0:T(8,128)(2,1)S(1)}, bf16[144,1024]{1,0:T(8,128)(2,1)}, u32[]{:S(2)}, u32[]{:S(2)}) collective-permute-start(bf16[144,1024]{1,0:T(8,128)(2,1)S(1)} %maximum_maximum_fusion), channel_id=1, source_target_pairs={{0,1},{1,0},{2,3},{3,2},{4,5},{5,4},{6,7},{7,6},{8,9},{9,8},{10,11... | collective-permute-start | bytes 884744 | tf_op jit(solution)/shard_map/ppermute | solution.py:29
  246.4 14.3 %collective-permute-start.17 = (bf16[4,64,256]{2,1,0:T(8,128)(2,1)S(1)}, bf16[4,64,256]{2,1,0:T(8,128)(2,1)S(1)}, u32[]{:S(2)}, u32[]{:S(2)}) collective-permute-start(bf16[4,64,256]{2,1,0:T(8,128)(2,1)S(1)} %reduce_sum.158), channel_id=1, source_target_pairs={{0,64},{32,96},{64,0},{96,32},{1,65},{33,97},{65,1},{97,33},{2,66}... | collective-permute-start | bytes 393224 | tf_op jit(solution)/shard_map/ppermute | solution.py:25
  248.4 19.6 %collective-permute-start.21 = (bf16[64,2304]{1,0:T(8,128)(2,1)S(1)}, bf16[64,2304]{1,0:T(8,128)(2,1)S(1)}, u32[]{:S(2)}, u32[]{:S(2)}) collective-permute-start(bf16[64,2304]{1,0:T(8,128)(2,1)S(1)} %copy-done.28), channel_id=1, source_target_pairs={{0,64},{32,96},{64,0},{96,32},{1,65},{33,97},{65,1},{97,33},{2,66}... | collective-permute-start | bytes 884744 | tf_op jit(solution)/shard_map/ppermute | solution.py:25
  260.8 9.2 %collective-permute-start.18 = (f32[4,64,256]{2,1,0:T(8,128)S(1)}, f32[4,64,256]{2,1,0:T(8,128)S(1)}, u32[]{:S(2)}, u32[]{:S(2)}) collective-permute-start(f32[4,64,256]{2,1,0:T(8,128)S(1)} %convert_add_fusion.3), channel_id=1, source_target_pairs={{0,32},{32,0},{64,96},{96,64},{1,33},{33,1},{65,97},{97,65},{2,34}... | collective-permute-start | bytes 786440 | tf_op jit(solution)/shard_map/ppermute | solution.py:21
  263.2 3.8 %collective-permute-start.23 = (f32[256]{0:T(256)S(1)}, f32[256]{0:T(256)S(1)}, u32[]{:S(2)}, u32[]{:S(2)}) collective-permute-start(f32[256]{0:T(256)S(1)} %bitcast.277), channel_id=1, source_target_pairs={{0,64},{32,96},{64,0},{96,32},{1,65},{33,97},{65,1},{97,33},{2,66}... | collective-permute-start | bytes 3080 | tf_op jit(solution)/shard_map/ppermute | solution.py:25
  264.4 7.9 %collective-permute-start.16 = (f32[2,32,1024]{2,1,0:T(8,128)S(1)}, f32[2,32,1024]{2,1,0:T(8,128)S(1)}, u32[]{:S(2)}, u32[]{:S(2)}) collective-permute-start(f32[2,32,1024]{2,1,0:T(8,128)S(1)} %dynamic-slice_bitcast_fusion), channel_id=1, source_target_pairs={{0,32},{32,0},{64,96},{96,64},{1,33},{33,1},{65,97},{97,65},{2,34}... | collective-permute-start | bytes 786440 | tf_op jit(solution)/shard_map/ppermute | solution.py:21
  267.1 1.7 collective-permute-start.24
  268.8 6.2 %collective-permute-start.22 = (f32[64,2304]{1,0:T(8,128)}, f32[64,2304]{1,0:T(8,128)}, u32[]{:S(2)}, u32[]{:S(2)}) collective-permute-start(f32[64,2304]{1,0:T(8,128)} %convert_add_fusion), channel_id=1, source_target_pairs={{0,32},{32,0},{64,96},{96,64},{1,33},{33,1},{65,97},{97,65},{2,34}... | collective-permute-start | bytes 1769480 | tf_op jit(solution)/shard_map/ppermute | solution.py:21
  (63 other events, 298.3 us)
Sparse Core Ops, SparseCore 0:
  14.6 80.0 all-gather.1
  126.3 89.5 reduce-scatter.1

commit v2 on v1

--- a/solution.py
+++ b/solution.py
@@ -508,8 +508,10 @@
     mlp_out = mm_nt(act, down_wt)
     out_tokens = hidden_mid + pair_sum(mlp_out[:128], mlp_out[128:])
     out_w_grad = mm_tn(grad_low, mixed).astype(bf16)
-    out_w_grad = exchange(after(out_w_grad, returned).reshape(16, 64, 512))
-    returned, mlp_w_grad = lax.optimization_barrier((returned, mlp_w_grad))
+    returned, mlp_w_grad, out_w_grad, _ = lax.optimization_barrier(
+        (returned, mlp_w_grad, out_w_grad, out_tokens)
+    )
+    out_w_grad = exchange(out_w_grad.reshape(16, 64, 512))
     out_w_grad = jnp.sum(out_w_grad.astype(f32), 0).astype(bf16)
     in_sum = jnp.sum(returned[:, :32].reshape(4, 4, 32, D).astype(f32), 1).reshape(128, D)
     gain_sum = jnp.sum(returned[:, 48:].astype(f32), 0)

time: 287 us -> 265 us (0.923)
  waiting for transfers between devices: 102 us -> 79 us
  other arithmetic: 44.5 us -> 40 us
  matrix products: 11.2 us -> 14.3 us
    all_to_all x4, waiting for transfers between devices: 65.7 us -> 46.6 us  [exchange(): return lax.all_to_all(values, 'ctx', 0, 0, tiled=True)]
    ppermute x4, waiting for transfers between devices: 16.2 us -> 2.29 us  [zlo_swap(): return lax.ppermute(values, 'rep', [(0, 2), (1, 3), (2, 0), (3, 1)])]
    ppermute x4, waiting for transfers between devices: 8.51 us -> 17.2 us  [tp_swap(): return lax.ppermute(values, 'tp', [(0, 1), (1, 0)])]
    unnamed x143 -> x145, local copies, waits for them, and re-layouts: 12 us -> 12.1 us
  transfers between devices with their start and end apart: 31 -> 31, of which waited for: 17 -> 18; matrix products, arithmetic and copies ran while one was open for 18% -> 19% of each run, Pallas kernels for 6% -> 6%
where the time goes in v2:
time: 265 us; the launch traced here: 263 us
  waiting for transfers between devices  79 us (30%)
  starting transfers between devices  57.8 us (22%)
  other arithmetic  40 us (15%)
  local copies, waits for them, and re-layouts  25.1 us (9%)
  Pallas kernels  18.3 us (7%)
  between operations  15.4 us (6%)
  matrix products  14.3 us (5%)
  blocking collectives  13.5 us (5%)
    all_to_all x4, waiting for transfers between devices, exchange(): return lax.all_to_all(values, 'ctx', 0, 0, tiled=True)  46.6 us
    ppermute x17, starting transfers between devices, core_swap(): return lax.ppermute(values, 'rep', [(0, 1), (1, 0), (2, 3), (3, 2)])  24.1 us
    all_to_all x4, starting transfers between devices, exchange(): return lax.all_to_all(values, 'ctx', 0, 0, tiled=True)  20.1 us
    pallas_call x5, Pallas kernels, kernel_call_scratch(): pl.pallas_call(body, out_shape=out_shape, in_specs=specs, out_specs=[pl.B...  18.3 us
    ppermute x4, waiting for transfers between devices, tp_swap(): return lax.ppermute(values, 'tp', [(0, 1), (1, 0)])  17.2 us
    all_to_all x1, blocking collectives, exchange(): return lax.all_to_all(values, 'ctx', 0, 0, tiled=True)  13.5 us
    unnamed x145, local copies, waits for them, and re-layouts  12.1 us
    ppermute x4, starting transfers between devices, tp_swap(): return lax.ppermute(values, 'tp', [(0, 1), (1, 0)])  11.6 us
  transfers between devices with their start and end apart: 31, of which 18 were waited for; matrix products, arithmetic and copies ran while one was open for 19% of the time, Pallas kernels for 6%

profile of v2, /device:TPU:1, one launch (start us, length us, event | category | flops | bytes accessed | tf_op | source)
XLA Modules:
  0.0 263.4 jit_solution(15080202115166433802)
XLA Ops:
  16.6 7.0 %all-to-all-start = ((bf16[16,56,1024]{2,1,0:T(8,128)(2,1)}), bf16[16,56,1024]{2,1,0:T(8,128)(2,1)S(1)}, u32[]{:S(2)}, u32[]{:S(2)}) async-start(bf16[16,56,1024]{2,1,0:T(8,128)(2,1)} %pad_maximum_fusion.1), calls=%async_computation | async-start | bytes 3670016 | tf_op jit(solution)/shard_map/all_to_all | solution.py:33
  28.1 3.1 %fusion.58 = (f32[1024,64]{1,0:T(8,128)}, f32[1024,64]{1,0:T(8,128)}, f32[1024,64]{1,0:T(8,128)}) fusion(f32[64]{0:T(128)S(1)} %multiply_exponential_fusion, f32[1024]{0:T(1024)S(1)} %subtract_convert_fusion), kind=kLoop, calls=%fused_computation.130 | loop fusion | flops 131072 | bytes 790784 | tf_op jit(solution)/shard_map/neg | solution.py:253
  31.2 22.7 %all-to-all-done = bf16[16,56,1024]{2,1,0:T(8,128)(2,1)S(1)} async-done(((bf16[16,56,1024]{2,1,0:T(8,128)(2,1)}), bf16[16,56,1024]{2,1,0:T(8,128)(2,1)S(1)}, u32[]{:S(2)}, u32[]{:S(2)}) %all-to-all-start) | async-done | bytes 1835040 | tf_op jit(solution)/shard_map/all_to_all | solution.py:33
  55.1 3.3 %collective-permute-start.1 = (bf16[16,32,1024]{2,1,0:T(8,128)(2,1)}, bf16[16,32,1024]{2,1,0:T(8,128)(2,1)}, u32[]{:S(2)}, u32[]{:S(2)}) collective-permute-start(bf16[16,32,1024]{2,1,0:T(8,128)(2,1)} %slice.432.tokens_ref), channel_id=1, source_target_pairs={{0,32},{32,0},{64,96},{96,64},{1,33},{33,1},{65,97},{97,65},{2,34}... | collective-permute-start | bytes 3145736 | tf_op jit(solution)/shard_map/ppermute | solution.py:21
  70.5 2.1 fusion.22.q_ref
  72.6 2.3 shard_map.237
  75.6 13.5 %all_to_all.25 = bf16[16,64,128]{2,1,0:T(8,128)(2,1)S(1)} all-to-all(bf16[16,64,128]{2,1,0:T(8,128)(2,1)S(1)} %bitcast.240), channel_id=1, replica_groups=mesh['rep'=4,'ctx'=16,'tp'=2] {'ctx'}, dimensions={0} | all-to-all | bytes 524288 | tf_op jit(solution)/shard_map/all_to_all | solution.py:33
  89.8 4.9 %all-gather.2.cloned.1.call-done = bf16[1024,2816]{1,0:T(8,128)(2,1)} async-done(((bf16[64,2816]{1,0:T(8,128)(2,1)}), bf16[1024,2816]{1,0:T(8,128)(2,1)}) %all-gather.2.cloned.1.call-update) | async-done | bytes 5767184 | tf_op jit(solution)/shard_map/all_gather | solution.py:351
  98.6 3.0 %collective-permute-start.6 = (bf16[128,1024]{1,0:T(8,128)(2,1)S(1)}, bf16[128,1024]{1,0:T(8,128)(2,1)}, u32[]{:S(2)}, u32[]{:S(2)}) collective-permute-start(bf16[128,1024]{1,0:T(8,128)(2,1)S(1)} %fusion.29), channel_id=1, source_target_pairs={{0,1},{1,0},{2,3},{3,2},{4,5},{5,4},{6,7},{7,6},{8,9},{9,8},{10,11... | collective-permute-start | bytes 786440 | tf_op jit(solution)/shard_map/ppermute | solution.py:29
  102.3 5.5 %collective-permute-done.6 = bf16[128,1024]{1,0:T(8,128)(2,1)} collective-permute-done((bf16[128,1024]{1,0:T(8,128)(2,1)S(1)}, bf16[128,1024]{1,0:T(8,128)(2,1)}, u32[]{:S(2)}, u32[]{:S(2)}) %collective-permute-start.6) | collective-permute-done | bytes 262176 | tf_op jit(solution)/shard_map/ppermute | solution.py:29
  111.9 3.0 %fusion.5 = f32[256,1536]{1,0:T(8,128)S(1)} fusion(bf16[1024,2816]{1,0:T(8,128)(2,1)} %all-gather.2.cloned.1.call-done, bf16[128,1024]{1,0:T(8,128)(2,1)} %collective-permute-done.7, bf16[128,1024]{1,0:T(8,128)(2,1)S(1)} %multiply_convert_fusion.3), kind=kOutput, calls=%fused_computation.7 | convolution fusion | flops 806354944 | bytes 5242880 | tf_op jit(solution)/shard_map/dot_general | solution.py:37
  114.9 2.2 multiply_convert_fusion.1
  118.5 3.7 %shard_map.238 = bf16[1024,2304]{1,0:T(8,128)(2,1)} custom-call(s32[1]{0:T(128)} %bitcast.50.unused, bf16[256,1024]{1,0:T(8,128)(2,1)S(1)} %pad_maximum_fusion.9.in_ref, bf16[256,1536]{1,0:T(8,128)(2,1)S(1)} %pad_maximum_fusion.4.up_ref, bf16[256,1024]{1,0:T(8,128)(2,1)S(1)} %pad_maximum_fusion.8.cot_ref, bf16[256,768]{1,0:T(8,128)(2,1)S(1)} %get-tuple-element.52.act_ref), custom_call_target="tpu_custom_call" | custom-call | flops 1207959552 | bytes 6946820 | tf_op jit(solution)/shard_map/pallas_call | solution.py:76
  123.1 3.0 %fusion.3 = f32[256,1024]{1,0:T(8,128)S(1)} fusion(bf16[1024,2816]{1,0:T(8,128)(2,1)} %all-gather.2.cloned.1.call-done, bf16[256,768]{1,0:T(8,128)(2,1)} %copy-done.32, bf16[256,768]{1,0:T(8,128)(2,1)S(1)} %copy-done.31), kind=kOutput, calls=%fused_computation.5 | convolution fusion | flops 806879232 | bytes 4980736 | tf_op jit(solution)/shard_map/dot_general | solution.py:41
  127.9 3.0 %collective-permute-start.9 = (bf16[128,1024]{1,0:T(8,128)(2,1)S(1)}, bf16[128,1024]{1,0:T(8,128)(2,1)S(1)}, u32[]{:S(2)}, u32[]{:S(2)}) collective-permute-start(bf16[128,1024]{1,0:T(8,128)(2,1)S(1)} %fusion.20), channel_id=1, source_target_pairs={{0,1},{1,0},{2,3},{3,2},{4,5},{5,4},{6,7},{7,6},{8,9},{9,8},{10,11... | collective-permute-start | bytes 786440 | tf_op jit(solution)/shard_map/ppermute | solution.py:29
  130.9 6.2 %collective-permute-done.9 = bf16[128,1024]{1,0:T(8,128)(2,1)S(1)} collective-permute-done((bf16[128,1024]{1,0:T(8,128)(2,1)S(1)}, bf16[128,1024]{1,0:T(8,128)(2,1)S(1)}, u32[]{:S(2)}, u32[]{:S(2)}) %collective-permute-start.9) | collective-permute-done | bytes 262176 | tf_op jit(solution)/shard_map/ppermute | solution.py:29
  143.3 5.0 %all-to-all-start.2 = ((bf16[16,64,128]{2,1,0:T(8,128)(2,1)}), bf16[16,64,128]{2,1,0:T(8,128)(2,1)}, u32[]{:S(2)}, u32[]{:S(2)}) async-start(bf16[16,64,128]{2,1,0:T(8,128)(2,1)} %shard_map.239), calls=%async_computation.2 | async-start | bytes 524288 | tf_op jit(solution)/shard_map/all_to_all | solution.py:33
  148.3 2.0 pad_maximum_fusion.3.rope_ref
  150.4 7.8 %all-to-all-done.2 = bf16[16,64,128]{2,1,0:T(8,128)(2,1)} async-done(((bf16[16,64,128]{2,1,0:T(8,128)(2,1)}), bf16[16,64,128]{2,1,0:T(8,128)(2,1)}, u32[]{:S(2)}, u32[]{:S(2)}) %all-to-all-start.2) | async-done | bytes 262176 | tf_op jit(solution)/shard_map/all_to_all | solution.py:33
  160.2 4.8 %shard_map.240 = (f32[1024,128]{1,0:T(8,128)S(1)}, f32[1024,128]{1,0:T(8,128)}, bf16[1024,128]{1,0:T(8,128)(2,1)S(1)}, f32[1,128]{1,0:T(1,128)S(1)}) custom-call(s32[1]{0:T(128)} %bitcast.1.odd.unused, bf16[1024,128]{1,0:T(8,128)(2,1)S(1)} %fusion.22.q_ref, bf16[1024,128]{1,0:T(8,128)(2,1)S(1)} %fusion.25.own_ref, bf16[1024,128]{1,0:T(8,128)(2,1)S(1)} %copy-done.5, ...), custom_call_target="tpu_custom_call" | custom-call | flops 838860800 | bytes 4469764 | tf_op jit(solution)/shard_map/pallas_call | solution.py:76
  172.4 6.4 %shard_map.241 = (f32[16,32,1024]{2,1,0:T(8,128)}, bf16[16,32,1024]{2,1,0:T(8,128)(2,1)}, bf16[16,16,1024]{2,1,0:T(8,128)(2,1)S(1)}, f32[1,1024]{1,0:T(1,128)S(1)}, f32[1,128]{1,0:T(1,128)S(1)}) custom-call(s32[1]{0:T(128)} %bitcast.1.odd.unused, f32[1024,128]{1,0:T(8,128)S(1)} %copy-done.7, f32[1024,128]{1,0:T(8,128)S(1)} %collective-permute-done.11.got_ref, ...), custom_call_target="tpu_custom_call" | custom-call | flops 1073741824 | bytes 9708548 | tf_op jit(solution)/shard_map/pallas_call | solution.py:76
  185.7 3.7 %all-to-all-start.3 = ((bf16[16,56,1024]{2,1,0:T(8,128)(2,1)}), bf16[16,56,1024]{2,1,0:T(8,128)(2,1)S(1)}, u32[]{:S(2)}, u32[]{:S(2)}) async-start(bf16[16,56,1024]{2,1,0:T(8,128)(2,1)} %pad_maximum_fusion.2), calls=%async_computation.3 | async-start | bytes 3670016 | tf_op jit(solution)/shard_map/all_to_all | solution.py:33
  189.5 2.1 fusion.7
  193.3 3.0 %collective-permute-start.14 = (bf16[128,1024]{1,0:T(8,128)(2,1)S(1)}, bf16[128,1024]{1,0:T(8,128)(2,1)S(1)}, u32[]{:S(2)}, u32[]{:S(2)}) collective-permute-start(bf16[128,1024]{1,0:T(8,128)(2,1)S(1)} %fusion.14), channel_id=1, source_target_pairs={{0,1},{1,0},{2,3},{3,2},{4,5},{5,4},{6,7},{7,6},{8,9},{9,8},{10,11... | collective-permute-start | bytes 786440 | tf_op jit(solution)/shard_map/ppermute | solution.py:29
  197.9 4.6 %collective-permute-done.14 = bf16[128,1024]{1,0:T(8,128)(2,1)S(1)} collective-permute-done((bf16[128,1024]{1,0:T(8,128)(2,1)S(1)}, bf16[128,1024]{1,0:T(8,128)(2,1)S(1)}, u32[]{:S(2)}, u32[]{:S(2)}) %collective-permute-start.14) | collective-permute-done | bytes 262176 | tf_op jit(solution)/shard_map/ppermute | solution.py:29
  203.3 16.1 %all-to-all-done.3 = bf16[16,56,1024]{2,1,0:T(8,128)(2,1)S(1)} async-done(((bf16[16,56,1024]{2,1,0:T(8,128)(2,1)}), bf16[16,56,1024]{2,1,0:T(8,128)(2,1)S(1)}, u32[]{:S(2)}, u32[]{:S(2)}) %all-to-all-start.3) | async-done | bytes 1835040 | tf_op jit(solution)/shard_map/all_to_all | solution.py:33
  221.2 2.7 %collective-permute-start.15 = (bf16[144,1024]{1,0:T(8,128)(2,1)S(1)}, bf16[144,1024]{1,0:T(8,128)(2,1)S(1)}, u32[]{:S(2)}, u32[]{:S(2)}) collective-permute-start(bf16[144,1024]{1,0:T(8,128)(2,1)S(1)} %maximum_maximum_fusion), channel_id=1, source_target_pairs={{0,1},{1,0},{2,3},{3,2},{4,5},{5,4},{6,7},{7,6},{8,9},{9,8},{10,11... | collective-permute-start | bytes 884744 | tf_op jit(solution)/shard_map/ppermute | solution.py:29
  224.0 4.4 %all-to-all-start.4 = ((bf16[16,64,512]{2,1,0:T(8,128)(2,1)}), bf16[16,64,512]{2,1,0:T(8,128)(2,1)}, u32[]{:S(2)}, u32[]{:S(2)}) async-start(bf16[16,64,512]{2,1,0:T(8,128)(2,1)} %bitcast.255), calls=%async_computation.5 | async-start | bytes 2097152 | tf_op jit(solution)/shard_map/all_to_all | solution.py:33
  228.5 2.5 collective-permute-start.18
  232.7 4.5 %collective-permute-start.16 = (f32[2,32,1024]{2,1,0:T(8,128)S(1)}, f32[2,32,1024]{2,1,0:T(8,128)S(1)}, u32[]{:S(2)}, u32[]{:S(2)}) collective-permute-start(f32[2,32,1024]{2,1,0:T(8,128)S(1)} %dynamic-slice_bitcast_fusion), channel_id=1, source_target_pairs={{0,32},{32,0},{64,96},{96,64},{1,33},{33,1},{65,97},{97,65},{2,34}... | collective-permute-start | bytes 786440 | tf_op jit(solution)/shard_map/ppermute | solution.py:21
  237.3 3.1 %collective-permute-start.24 = (f32[256]{0:T(256)S(1)}, f32[256]{0:T(256)S(1)}, u32[]{:S(2)}, u32[]{:S(2)}) collective-permute-start(f32[256]{0:T(256)S(1)} %add.170), channel_id=1, source_target_pairs={{0,32},{32,0},{64,96},{96,64},{1,33},{33,1},{65,97},{97,65},{2,34}... | collective-permute-start | bytes 3080 | tf_op jit(solution)/shard_map/ppermute | solution.py:21
  250.7 2.3 collective-permute-done.19
  (322 shorter events, 84.5 us)
Async XLA Ops:
  7.3 87.4 %all-gather.2.cloned.1.call-start = ((), (), s32[]{:S(2)}) async-start(), calls=%async_computation.6 | async-start | bytes 6127616 | tf_op jit(solution)/shard_map/all_gather | solution.py:351
  8.3 2.5 collective-permute-start
  16.6 37.3 %all-to-all-start = ((bf16[16,56,1024]{2,1,0:T(8,128)(2,1)}), bf16[16,56,1024]{2,1,0:T(8,128)(2,1)S(1)}, u32[]{:S(2)}, u32[]{:S(2)}) async-start(bf16[16,56,1024]{2,1,0:T(8,128)(2,1)} %pad_maximum_fusion.1), calls=%async_computation | async-start | bytes 3670016 | tf_op jit(solution)/shard_map/all_to_all | solution.py:33
  23.6 195.8 %reduce-scatter.2.cloned.1.call-start = ((), (), s32[]{:S(2)}) async-start(), calls=%async_computation.7 | async-start | bytes 5013504 | tf_op jit(solution)/shard_map/reduce_scatter | solution.py:435
  23.6 1.6 collective-permute-start.2
  24.4 34.1 %collective-permute-start.4 = (bf16[128,1024]{1,0:T(8,128)(2,1)S(1)}, bf16[128,1024]{1,0:T(8,128)(2,1)S(1)}, u32[]{:S(2)}, u32[]{:S(2)}) collective-permute-start(bf16[128,1024]{1,0:T(8,128)(2,1)S(1)} %bitcast.245), channel_id=1, source_target_pairs={{0,32},{32,0},{64,96},{96,64},{1,33},{33,1},{65,97},{97,65},{2,34}... | collective-permute-start | bytes 786440 | tf_op jit(solution)/shard_map/ppermute | solution.py:21
  55.1 7.9 %collective-permute-start.1 = (bf16[16,32,1024]{2,1,0:T(8,128)(2,1)}, bf16[16,32,1024]{2,1,0:T(8,128)(2,1)}, u32[]{:S(2)}, u32[]{:S(2)}) collective-permute-start(bf16[16,32,1024]{2,1,0:T(8,128)(2,1)} %slice.432.tokens_ref), channel_id=1, source_target_pairs={{0,32},{32,0},{64,96},{96,64},{1,33},{33,1},{65,97},{97,65},{2,34}... | collective-permute-start | bytes 3145736 | tf_op jit(solution)/shard_map/ppermute | solution.py:21
  69.7 2.9 %collective-permute-start.3 = (bf16[1024,128]{1,0:T(8,128)(2,1)S(1)}, bf16[1024,128]{1,0:T(8,128)(2,1)S(1)}, u32[]{:S(2)}, u32[]{:S(2)}) collective-permute-start(bf16[1024,128]{1,0:T(8,128)(2,1)S(1)} %fusion.25.own_ref), channel_id=1, source_target_pairs={{0,32},{32,0},{64,96},{96,64},{1,33},{33,1},{65,97},{97,65},{2,34}... | collective-permute-start | bytes 786440 | tf_op jit(solution)/shard_map/ppermute | solution.py:21
  96.6 1.9 collective-permute-start.5
  98.6 9.2 %collective-permute-start.6 = (bf16[128,1024]{1,0:T(8,128)(2,1)S(1)}, bf16[128,1024]{1,0:T(8,128)(2,1)}, u32[]{:S(2)}, u32[]{:S(2)}) collective-permute-start(bf16[128,1024]{1,0:T(8,128)(2,1)S(1)} %fusion.29), channel_id=1, source_target_pairs={{0,1},{1,0},{2,3},{3,2},{4,5},{5,4},{6,7},{7,6},{8,9},{9,8},{10,11... | collective-permute-start | bytes 786440 | tf_op jit(solution)/shard_map/ppermute | solution.py:29
  102.3 35.6 %copy-start.36 = (f32[1024]{0:T(1024)}, f32[1024]{0:T(1024)S(1)}, u32[]{:S(2)}) copy-start(f32[1024]{0:T(1024)S(1)} %mul.284) | copy-start | bytes 12292
  109.2 2.8 %collective-permute-start.7 = (bf16[128,1024]{1,0:T(8,128)(2,1)S(1)}, bf16[128,1024]{1,0:T(8,128)(2,1)}, u32[]{:S(2)}, u32[]{:S(2)}) collective-permute-start(bf16[128,1024]{1,0:T(8,128)(2,1)S(1)} %multiply_convert_fusion.3), channel_id=1, source_target_pairs={{0,32},{32,0},{64,96},{96,64},{1,33},{33,1},{65,97},{97,65},{2,34}... | collective-permute-start | bytes 786440 | tf_op jit(solution)/shard_map/ppermute | solution.py:21
  126.2 1.6 collective-permute-start.8
  127.9 9.1 %collective-permute-start.9 = (bf16[128,1024]{1,0:T(8,128)(2,1)S(1)}, bf16[128,1024]{1,0:T(8,128)(2,1)S(1)}, u32[]{:S(2)}, u32[]{:S(2)}) collective-permute-start(bf16[128,1024]{1,0:T(8,128)(2,1)S(1)} %fusion.20), channel_id=1, source_target_pairs={{0,1},{1,0},{2,3},{3,2},{4,5},{5,4},{6,7},{7,6},{8,9},{9,8},{10,11... | collective-permute-start | bytes 786440 | tf_op jit(solution)/shard_map/ppermute | solution.py:29
  138.6 2.6 collective-permute-start.10
  143.3 15.0 %all-to-all-start.2 = ((bf16[16,64,128]{2,1,0:T(8,128)(2,1)}), bf16[16,64,128]{2,1,0:T(8,128)(2,1)}, u32[]{:S(2)}, u32[]{:S(2)}) async-start(bf16[16,64,128]{2,1,0:T(8,128)(2,1)} %shard_map.239), calls=%async_computation.2 | async-start | bytes 524288 | tf_op jit(solution)/shard_map/all_to_all | solution.py:33
  166.5 2.9 %collective-permute-start.11 = (f32[1024,128]{1,0:T(8,128)}, f32[1024,128]{1,0:T(8,128)S(1)}, u32[]{:S(2)}, u32[]{:S(2)}) collective-permute-start(f32[1024,128]{1,0:T(8,128)} %get-tuple-element.44), channel_id=1, source_target_pairs={{0,32},{32,0},{64,96},{96,64},{1,33},{33,1},{65,97},{97,65},{2,34}... | collective-permute-start | bytes 1572872 | tf_op jit(solution)/shard_map/ppermute | solution.py:21
  179.4 2.9 %collective-permute-start.12 = (bf16[16,32,1024]{2,1,0:T(8,128)(2,1)}, bf16[16,32,1024]{2,1,0:T(8,128)(2,1)S(1)}, u32[]{:S(2)}, u32[]{:S(2)}) collective-permute-start(bf16[16,32,1024]{2,1,0:T(8,128)(2,1)} %get-tuple-element.47), channel_id=1, source_target_pairs={{0,32},{32,0},{64,96},{96,64},{1,33},{33,1},{65,97},{97,65},{2,34}... | collective-permute-start | bytes 3145736 | tf_op jit(solution)/shard_map/ppermute | solution.py:21
  185.7 33.7 %all-to-all-start.3 = ((bf16[16,56,1024]{2,1,0:T(8,128)(2,1)}), bf16[16,56,1024]{2,1,0:T(8,128)(2,1)S(1)}, u32[]{:S(2)}, u32[]{:S(2)}) async-start(bf16[16,56,1024]{2,1,0:T(8,128)(2,1)} %pad_maximum_fusion.2), calls=%async_computation.3 | async-start | bytes 3670016 | tf_op jit(solution)/shard_map/all_to_all | solution.py:33
  191.6 1.6 collective-permute-start.13
  193.3 9.1 %collective-permute-start.14 = (bf16[128,1024]{1,0:T(8,128)(2,1)S(1)}, bf16[128,1024]{1,0:T(8,128)(2,1)S(1)}, u32[]{:S(2)}, u32[]{:S(2)}) collective-permute-start(bf16[128,1024]{1,0:T(8,128)(2,1)S(1)} %fusion.14), channel_id=1, source_target_pairs={{0,1},{1,0},{2,3},{3,2},{4,5},{5,4},{6,7},{7,6},{8,9},{9,8},{10,11... | collective-permute-start | bytes 786440 | tf_op jit(solution)/shard_map/ppermute | solution.py:29
  219.9 8.5 %collective-permute-start.17 = (bf16[4,64,256]{2,1,0:T(8,128)(2,1)S(1)}, bf16[4,64,256]{2,1,0:T(8,128)(2,1)S(1)}, u32[]{:S(2)}, u32[]{:S(2)}) collective-permute-start(bf16[4,64,256]{2,1,0:T(8,128)(2,1)S(1)} %reduce_sum.158), channel_id=1, source_target_pairs={{0,64},{32,96},{64,0},{96,32},{1,65},{33,97},{65,1},{97,33},{2,66}... | collective-permute-start | bytes 393224 | tf_op jit(solution)/shard_map/ppermute | solution.py:25
  221.2 10.8 %collective-permute-start.15 = (bf16[144,1024]{1,0:T(8,128)(2,1)S(1)}, bf16[144,1024]{1,0:T(8,128)(2,1)S(1)}, u32[]{:S(2)}, u32[]{:S(2)}) collective-permute-start(bf16[144,1024]{1,0:T(8,128)(2,1)S(1)} %maximum_maximum_fusion), channel_id=1, source_target_pairs={{0,1},{1,0},{2,3},{3,2},{4,5},{5,4},{6,7},{7,6},{8,9},{9,8},{10,11... | collective-permute-start | bytes 884744 | tf_op jit(solution)/shard_map/ppermute | solution.py:29
  224.0 24.4 %all-to-all-start.4 = ((bf16[16,64,512]{2,1,0:T(8,128)(2,1)}), bf16[16,64,512]{2,1,0:T(8,128)(2,1)}, u32[]{:S(2)}, u32[]{:S(2)}) async-start(bf16[16,64,512]{2,1,0:T(8,128)(2,1)} %bitcast.255), calls=%async_computation.5 | async-start | bytes 2097152 | tf_op jit(solution)/shard_map/all_to_all | solution.py:33
  228.3 12.1 %collective-permute-start.21 = (bf16[64,2304]{1,0:T(8,128)(2,1)S(1)}, bf16[64,2304]{1,0:T(8,128)(2,1)S(1)}, u32[]{:S(2)}, u32[]{:S(2)}) collective-permute-start(bf16[64,2304]{1,0:T(8,128)(2,1)S(1)} %copy-done.26), channel_id=1, source_target_pairs={{0,64},{32,96},{64,0},{96,32},{1,65},{33,97},{65,1},{97,33},{2,66}... | collective-permute-start | bytes 884744 | tf_op jit(solution)/shard_map/ppermute | solution.py:25
  228.5 14.0 %collective-permute-start.18 = (f32[4,64,256]{2,1,0:T(8,128)S(1)}, f32[4,64,256]{2,1,0:T(8,128)S(1)}, u32[]{:S(2)}, u32[]{:S(2)}) collective-permute-start(f32[4,64,256]{2,1,0:T(8,128)S(1)} %convert_add_fusion.3), channel_id=1, source_target_pairs={{0,32},{32,0},{64,96},{96,64},{1,33},{33,1},{65,97},{97,65},{2,34}... | collective-permute-start | bytes 786440 | tf_op jit(solution)/shard_map/ppermute | solution.py:21
  232.2 5.1 %collective-permute-start.23 = (f32[256]{0:T(256)S(1)}, f32[256]{0:T(256)S(1)}, u32[]{:S(2)}, u32[]{:S(2)}) collective-permute-start(f32[256]{0:T(256)S(1)} %bitcast.277), channel_id=1, source_target_pairs={{0,64},{32,96},{64,0},{96,32},{1,65},{33,97},{65,1},{97,33},{2,66}... | collective-permute-start | bytes 3080 | tf_op jit(solution)/shard_map/ppermute | solution.py:25
  232.7 12.0 %collective-permute-start.16 = (f32[2,32,1024]{2,1,0:T(8,128)S(1)}, f32[2,32,1024]{2,1,0:T(8,128)S(1)}, u32[]{:S(2)}, u32[]{:S(2)}) collective-permute-start(f32[2,32,1024]{2,1,0:T(8,128)S(1)} %dynamic-slice_bitcast_fusion), channel_id=1, source_target_pairs={{0,32},{32,0},{64,96},{96,64},{1,33},{33,1},{65,97},{97,65},{2,34}... | collective-permute-start | bytes 786440 | tf_op jit(solution)/shard_map/ppermute | solution.py:21
  237.3 4.0 %collective-permute-start.24 = (f32[256]{0:T(256)S(1)}, f32[256]{0:T(256)S(1)}, u32[]{:S(2)}, u32[]{:S(2)}) collective-permute-start(f32[256]{0:T(256)S(1)} %add.170), channel_id=1, source_target_pairs={{0,32},{32,0},{64,96},{96,64},{1,33},{33,1},{65,97},{97,65},{2,34}... | collective-permute-start | bytes 3080 | tf_op jit(solution)/shard_map/ppermute | solution.py:21
  241.3 5.1 %collective-permute-start.22 = (f32[64,2304]{1,0:T(8,128)}, f32[64,2304]{1,0:T(8,128)}, u32[]{:S(2)}, u32[]{:S(2)}) collective-permute-start(f32[64,2304]{1,0:T(8,128)} %convert_add_fusion), channel_id=1, source_target_pairs={{0,32},{32,0},{64,96},{96,64},{1,33},{33,1},{65,97},{97,65},{2,34}... | collective-permute-start | bytes 1769480 | tf_op jit(solution)/shard_map/ppermute | solution.py:21
  249.7 3.2 %collective-permute-start.19 = (bf16[64,512]{1,0:T(8,128)(2,1)S(1)}, bf16[64,512]{1,0:T(8,128)(2,1)S(1)}, u32[]{:S(2)}, u32[]{:S(2)}) collective-permute-start(bf16[64,512]{1,0:T(8,128)(2,1)S(1)} %reduce_sum.159), channel_id=1, source_target_pairs={{0,64},{32,96},{64,0},{96,32},{1,65},{33,97},{65,1},{97,33},{2,66}... | collective-permute-start | bytes 196616 | tf_op jit(solution)/shard_map/ppermute | solution.py:25
  253.0 2.7 %collective-permute-start.20 = (f32[64,512]{1,0:T(8,128)S(1)}, f32[64,512]{1,0:T(8,128)S(1)}, u32[]{:S(2)}, u32[]{:S(2)}) collective-permute-start(f32[64,512]{1,0:T(8,128)S(1)} %convert_add_fusion.4), channel_id=1, source_target_pairs={{0,32},{32,0},{64,96},{96,64},{1,33},{33,1},{65,97},{97,65},{2,34}... | collective-permute-start | bytes 393224 | tf_op jit(solution)/shard_map/ppermute | solution.py:21
  (64 other events, 315.8 us)
Sparse Core Ops, SparseCore 0:
  14.6 80.0 all-gather.1
  122.3 88.1 reduce-scatter.1
